TPU v7x, 128 devices: a whole 4x4x4 slice. The times are simulated.
128 devices in a mesh: seq: 32 (over z, y_lo, x), chan: 4 (over y_hi, core).
Axes of the slice: x: 4, y: 4 (y_hi: 2, y_lo: 2; y = y_hi * 2 + y_lo), z: 4, core: 2. Of those that a mesh axis runs over, the one named last changes fastest.
Arguments:
- layer_in: bfloat16 [16384, 2048], P('seq', 'chan')
- factor_one: bfloat16 [64, 256, 256], P('seq'), may hold values from -0.375 to 0.375
- factor_two: bfloat16 [256, 64, 64], P('seq'), may hold values from -0.75 to 0.75
- gate_scale: float32 [2048], P('chan'), may hold values from 0.5 to 2
- gate_shift: float32 [2048], P('chan'), may hold values from -3 to 3
- norm_gain: float32 [2048], replicated, may hold values from 0.1 to 1.9
- w_gate: bfloat16 [2048, 4096], P(None, 'chan'), may hold values from -0.125 to 0.125
- w_up: bfloat16 [2048, 4096], P(None, 'chan'), may hold values from -0.125 to 0.125
- w_down: bfloat16 [4096, 2048], P('chan'), may hold values from -0.09375 to 0.09375
- out_grad: bfloat16 [16384, 2048], P('seq', 'chan'), may hold values from -6 to 6
Outputs:
- layer_out: bfloat16 [16384, 2048], P('seq', 'chan')
- input_grad: bfloat16 [16384, 2048], P('seq', 'chan')
- one_grad: float32 [64, 256, 256], P('seq')
- two_grad: float32 [256, 64, 64], P('seq')
- scale_grad: float32 [2048], P('chan')
- shift_grad: float32 [2048], P('chan')
- gain_grad: float32 [2048], P('chan')
- gate_grad: float32 [2048, 4096], P('seq', 'chan')
- up_grad: float32 [2048, 4096], P('seq', 'chan')
- down_grad: float32 [4096, 2048], P('chan', 'seq')
All inputs are finite; a program needn't handle non-finite values.
Results may differ from a plain program's by a relative error of at most 0.015.
Values may be sent and summed in bfloat16 or wider, within the bound.
A program may use at most 192 MiB of HBM per device.

v0:
```python
import jax
import jax.numpy as jnp
from jax import lax
from jax.sharding import PartitionSpec as P


def on_device(
    layer_in,
    factor_one,
    factor_two,
    gate_scale,
    gate_shift,
    norm_gain,
    w_gate,
    w_up,
    w_down,
    out_grad,
):
    rows, width = layer_in.shape
    chan_count = lax.axis_size("chan")
    block_count = factor_one.shape[0]
    block = factor_one.shape[1]
    full_width = width * chan_count
    dims_first = (((0,), (0,)), ((), ()))
    in_float = layer_in.astype(jnp.float32)
    in_blocks = layer_in.reshape(block_count, block, width)
    first_local = jnp.einsum(
        "pkq,pqc->pkc", factor_one, in_blocks, preferred_element_type=jnp.float32
    ).astype(jnp.bfloat16)
    first_cols = lax.all_to_all(first_local, "seq", split_axis=1, concat_axis=0, tiled=True)
    second_cols = jnp.einsum(
        "qjp,pqc->jqc", factor_two, first_cols, preferred_element_type=jnp.float32
    ).astype(jnp.bfloat16)
    second_rows = lax.all_to_all(
        second_cols, "seq", split_axis=0, concat_axis=1, tiled=True
    ).reshape(rows, width)
    seqmix = second_rows.astype(jnp.float32)
    opening = jax.nn.sigmoid(in_float * gate_scale + gate_shift)
    mixed = (in_float + opening * seqmix).astype(jnp.bfloat16)
    mixed_float = mixed.astype(jnp.float32)
    whole = lax.all_gather(mixed, "chan", axis=1, tiled=True)
    whole_float = whole.astype(jnp.float32)
    inv_rms = lax.rsqrt(jnp.mean(whole_float * whole_float, axis=1, keepdims=True) + 1e-05)
    normed = (whole_float * inv_rms * norm_gain).astype(jnp.bfloat16)
    gate_pre = jnp.dot(normed, w_gate, preferred_element_type=jnp.float32)
    up_pre = jnp.dot(normed, w_up, preferred_element_type=jnp.float32)
    gate_sigmoid = jax.nn.sigmoid(gate_pre)
    hidden = (gate_pre * gate_sigmoid * up_pre).astype(jnp.bfloat16)
    mlp_cols = lax.psum_scatter(
        lax.dot_general(
            w_down, hidden, (((0,), (1,)), ((), ())), preferred_element_type=jnp.float32
        ).astype(jnp.bfloat16),
        "chan",
        scatter_dimension=0,
        tiled=True,
    ).astype(jnp.float32)
    layer_out = (mixed_float + mlp_cols.T).astype(jnp.bfloat16)
    offset = lax.axis_index("chan") * width
    gain_own = lax.dynamic_slice_in_dim(norm_gain, offset, width, 0)
    cot_whole = lax.all_gather(out_grad, "chan", axis=1, tiled=True)
    hidden_grad = lax.dot_general(
        cot_whole, w_down, (((1,), (1,)), ((), ())), preferred_element_type=jnp.float32
    )
    gate_back = (
        hidden_grad * up_pre * gate_sigmoid * (1.0 + gate_pre * (1.0 - gate_sigmoid))
    ).astype(jnp.bfloat16)
    up_back = (hidden_grad * gate_pre * gate_sigmoid).astype(jnp.bfloat16)
    hidden_width = gate_back.shape[1]
    gate_term = lax.dot_general(normed, gate_back, dims_first, preferred_element_type=jnp.float32)
    up_term = lax.dot_general(normed, up_back, dims_first, preferred_element_type=jnp.float32)
    joint_part = lax.psum_scatter(
        jnp.concatenate(
            [
                jnp.concatenate([gate_term, up_term], axis=1),
                lax.dot_general(cot_whole, hidden, dims_first, preferred_element_type=jnp.float32),
            ],
            axis=1,
        ),
        "seq",
        scatter_dimension=0,
        tiled=True,
    )
    gate_part = joint_part[:, :hidden_width]
    up_part = joint_part[:, hidden_width : 2 * hidden_width]
    down_part = joint_part[:, 2 * hidden_width :]
    contract = (((1,), (1,)), ((), ()))
    total = lax.dot_general(w_gate, gate_back, contract, preferred_element_type=jnp.float32)
    normed_grad = lax.psum_scatter(
        total + lax.dot_general(w_up, up_back, contract, preferred_element_type=jnp.float32),
        "chan",
        scatter_dimension=0,
        tiled=True,
    ).T
    row_local = jnp.sum(normed_grad * gain_own * mixed_float, axis=1, keepdims=True)
    row_dots = lax.psum(row_local, "chan")
    mixed_grad = out_grad.astype(jnp.float32) + inv_rms * gain_own * normed_grad
    mixed_grad = mixed_grad - mixed_float * inv_rms * inv_rms * inv_rms * row_dots / full_width
    gain_local = jnp.sum(normed_grad * mixed_float * inv_rms, axis=0)
    seqmix_grad = (mixed_grad * opening).astype(jnp.bfloat16)
    pre_grad = mixed_grad * seqmix * opening * (1.0 - opening)
    scale_local = jnp.sum(pre_grad * in_float, axis=0)
    shift_local = jnp.sum(pre_grad, axis=0)
    grad_cols = lax.all_to_all(
        seqmix_grad.reshape(block_count, block, width),
        "seq",
        split_axis=1,
        concat_axis=0,
        tiled=True,
    )
    first_grad_cols = jnp.einsum(
        "qjp,jqc->pqc", factor_two, grad_cols, preferred_element_type=jnp.float32
    ).astype(jnp.bfloat16)
    two_local = jnp.einsum(
        "jqc,pqc->qjp", grad_cols, first_cols, preferred_element_type=jnp.float32
    )
    first_grad_rows = lax.all_to_all(
        first_grad_cols, "seq", split_axis=0, concat_axis=1, tiled=True
    )
    input_part = jnp.einsum(
        "pkq,pkc->pqc", factor_one, first_grad_rows, preferred_element_type=jnp.float32
    ).reshape(rows, width)
    one_local = jnp.einsum(
        "pkc,pqc->pkq", first_grad_rows, in_blocks, preferred_element_type=jnp.float32
    )
    one_grad, two_grad = (
        lax.psum(one_local.astype(jnp.bfloat16), "chan").astype(jnp.float32),
        lax.psum(two_local.astype(jnp.bfloat16), "chan").astype(jnp.float32),
    )
    scale_grad, shift_grad, gain_grad = lax.psum((scale_local, shift_local, gain_local), "seq")
    input_grad = (mixed_grad + pre_grad * gate_scale + input_part).astype(jnp.bfloat16)
    return (
        layer_out,
        input_grad,
        one_grad,
        two_grad,
        scale_grad,
        shift_grad,
        gain_grad,
        gate_part,
        up_part,
        down_part.T,
    )


def solution(mesh):
    return jax.shard_map(
        on_device,
        mesh=mesh,
        in_specs=(
            P("seq", "chan"),
            P("seq", None, None),
            P("seq", None, None),
            P("chan"),
            P("chan"),
            P(),
            P(None, "chan"),
            P(None, "chan"),
            P("chan", None),
            P("seq", "chan"),
        ),
        out_specs=(
            P("seq", "chan"),
            P("seq", "chan"),
            P("seq", None, None),
            P("seq", None, None),
            P("chan"),
            P("chan"),
            P("chan"),
            P("seq", "chan"),
            P("seq", "chan"),
            P("chan", "seq"),
        ),
        check_vma=False,
    )
```

profile of v0, /device:TPU:16, one launch (start us, length us, event | category | flops | bytes accessed | tf_op | source)
XLA Modules:
  0.0 580.3 jit_solution(4232112637310719532)
XLA Ops:
  8.1 1.3 convolution_convert_fusion.3
  10.1 20.4 %all_to_all.63 = bf16[2,256,512]{2,0,1:T(2,128)(2,1)S(1)} all-to-all(bf16[2,256,512]{2,0,1:T(2,128)(2,1)S(1)} %copy.29), channel_id=1, replica_groups=mesh['seq'=32,'chan'=4] {'seq'}, dimensions={1} | all-to-all | bytes 1048576 | tf_op jit(solution)/shard_map/all_to_all | solution.py:30
  31.6 14.5 %all_to_all.64 = bf16[64,8,512]{2,1,0:T(8,128)(2,1)S(1)} all-to-all(bf16[64,8,512]{2,1,0:T(8,128)(2,1)S(1)} %copy.31), channel_id=1, replica_groups=mesh['seq'=32,'chan'=4] {'seq'}, dimensions={0} | all-to-all | bytes 1048576 | tf_op jit(solution)/shard_map/all_to_all | solution.py:34
  48.5 20.9 %all-gather.3.cloned.1.call-done = bf16[512,2048]{1,0:T(8,128)(2,1)} async-done(((bf16[512,512]{1,0:T(8,128)(2,1)}), bf16[512,2048]{1,0:T(8,128)(2,1)}) %all-gather.3.cloned.1.call-update) | async-done | bytes 2097168 | tf_op jit(solution)/shard_map/all_gather | solution.py:41
  69.4 2.1 fusion
  71.5 6.7 %fusion.35 = f32[512,1024]{1,0:T(8,128)} fusion(bf16[2048,1024]{1,0:T(8,128)(2,1)} %param.17, bf16[512,2048]{1,0:T(8,128)(2,1)} %all-gather.3.cloned.1.call-done, f32[2048]{0:T(1024)S(1)} %copy-done.15, f32[512]{0:T(512)S(1)} %add_rsqrt_fusion), kind=kOutput, calls=%fused_computation.65 | convolution fusion | flops 2151677952 | bytes 8398848 | tf_op jit(solution)/shard_map/dot_general | solution.py:46
  78.2 3.7 fusion.37
  81.9 15.2 %all-gather.5.cloned.1.call-done = bf16[512,2048]{1,0:T(8,128)(2,1)} async-done(((bf16[512,512]{1,0:T(8,128)(2,1)}), bf16[512,2048]{1,0:T(8,128)(2,1)}) %all-gather.5.cloned.1.call-update) | async-done | bytes 2097168 | tf_op jit(solution)/shard_map/all_gather | solution.py:60
  97.1 8.3 %multiply_convert_fusion = (bf16[512,1024]{1,0:T(8,128)(2,1)S(1)}, bf16[512,1024]{1,0:T(8,128)(2,1)S(1)}, bf16[512,1024]{1,0:T(8,128)(2,1)}) fusion(f32[512,1024]{1,0:T(8,128)} %fusion.37, f32[512,1024]{1,0:T(8,128)} %fusion.35, bf16[512,2048]{1,0:T(8,128)(2,1)} %all-gather.5.cloned.1.call-done, bf16[1024,2048]{1,0:T(8,128)(2,1)} %param.18), kind=kOutput, calls=%fused_computation.10 | convolution fusion | flops 2155872256 | bytes 13631488 | tf_op jit(solution)/shard_map/dot_general | solution.py:61
  105.4 2.4 fusion.42
  108.4 4.4 add_bitcast_fusion
  113.0 6.2 %fusion.3 = bf16[2048,512]{0,1:T(8,128)(2,1)} fusion(bf16[512,1024]{1,0:T(8,128)(2,1)} %get-tuple-element.43, bf16[1024,2048]{1,0:T(8,128)(2,1)} %param.18), kind=kOutput, calls=%fused_computation.9 | convolution fusion | flops 2148532224 | bytes 7340032 | tf_op jit(solution)/shard_map/dot_general | solution.py:50
  119.3 8.4 %fusion.31 = f32[2048,1024]{0,1:T(8,128)} fusion(bf16[512,1024]{1,0:T(8,128)(2,1)} %copy-done.20, bf16[512,2048]{1,0:T(8,128)(2,1)} %all-gather.3.cloned.1.call-done, f32[2048]{0:T(1024)S(1)} %copy-done.15, f32[512]{0:T(512)S(1)} %add_rsqrt_fusion), kind=kOutput, calls=%fused_computation.63 | convolution fusion | flops 2151677952 | bytes 11544576 | tf_op jit(solution)/shard_map/dot_general | solution.py:70
  127.7 36.0 %reduce-scatter.8.cloned.1.call-done = f32[512,512]{0,1:T(8,128)} async-done(((f32[2048,512]{0,1:T(8,128)}), f32[512,512]{0,1:T(8,128)}) %reduce-scatter.8.cloned.1.call-update) | async-done | bytes 1048592 | tf_op jit(solution)/shard_map/reduce_scatter | solution.py:88
  163.7 2.3 fusion.21
  166.0 10.7 %psum.42 = f32[512]{0:T(512)} all-reduce(f32[512]{0:T(512)S(1)} %get-tuple-element.31), channel_id=1, replica_groups=mesh['seq'=32,'chan'=4] {'chan'}, use_global_device_ids=true, to_apply=%region_4.0 | all-reduce | flops 512 | bytes 4096 | tf_op jit(solution)/shard_map/psum | solution.py:95
  176.7 27.5 %reduce-scatter.6.cloned.1.call-done = bf16[512,512]{0,1:T(8,128)(2,1)} async-done(((bf16[2048,512]{0,1:T(8,128)(2,1)}), bf16[512,512]{0,1:T(8,128)(2,1)}) %reduce-scatter.6.cloned.1.call-update) | async-done | bytes 524304 | tf_op jit(solution)/shard_map/reduce_scatter | solution.py:49
  204.2 4.3 fusion.39
  208.7 1.3 copy.33
  210.1 9.0 %all-to-all-start.2 = ((bf16[2,256,512]{2,0,1:T(2,128)(2,1)}), bf16[2,256,512]{2,0,1:T(2,128)(2,1)S(1)}, u32[]{:S(2)}, u32[]{:S(2)}) async-start(bf16[2,256,512]{2,0,1:T(2,128)(2,1)} %copy.33), calls=%async_computation.4 | async-start | bytes 1048576 | tf_op jit(solution)/shard_map/all_to_all | solution.py:103
  219.1 7.6 %fusion.33 = f32[2048,1024]{0,1:T(8,128)} fusion(bf16[512,1024]{1,0:T(8,128)(2,1)} %copy-done.19, bf16[512,2048]{1,0:T(8,128)(2,1)} %all-gather.3.cloned.1.call-done, f32[2048]{0:T(1024)} %param.15, f32[512]{0:T(512)S(1)} %add_rsqrt_fusion), kind=kOutput, calls=%fused_computation.64 | convolution fusion | flops 2151677952 | bytes 11544576 | tf_op jit(solution)/shard_map/dot_general | solution.py:69
  226.7 3.9 all-to-all-done.2
  232.7 4.4 all-to-all-start.3
  237.4 7.5 %convolution_bitcast_fusion = f32[2048,1024]{0,1:T(8,128)} fusion(bf16[512,1024]{1,0:T(8,128)(2,1)} %get-tuple-element.43, bf16[512,2048]{1,0:T(8,128)(2,1)} %all-gather.5.cloned.1.call-done), kind=kOutput, calls=%fused_computation.3 | convolution fusion | flops 2147483648 | bytes 11534336 | tf_op jit(solution)/shard_map/dot_general | solution.py:75
  245.8 2.2 all-to-all-done.3
  249.2 18.4 %pad_maximum_fusion = f32[2048,3072]{0,1:T(8,128)} fusion(f32[2048,1024]{0,1:T(8,128)} %convolution_bitcast_fusion, f32[2048,1024]{0,1:T(8,128)} %fusion.31, f32[2048,1024]{0,1:T(8,128)} %fusion.33), kind=kLoop, calls=%fused_computation | loop fusion | flops 12582912 | bytes 50331648 | tf_op jit(solution)/shard_map/concatenate | solution.py:72
  267.6 24.7 %copy.44 = f32[2048,3072]{1,0:T(8,128)} copy(f32[2048,3072]{0,1:T(8,128)} %pad_maximum_fusion) | data formatting | bytes 50331648
  293.0 85.1 %all-reduce = (f32[512]{0:T(512)}, f32[512]{0:T(512)}, f32[512]{0:T(512)}) all-reduce(f32[512]{0:T(512)S(1)} %copy-done.14, f32[512]{0:T(512)S(1)} %copy-done.13, f32[512]{0:T(512)S(1)} %copy-done.12), channel_id=1, replica_groups=mesh['seq'=32,'chan'=4] {'seq'}, use_global_device_ids=true, to_apply=%region_8.0 | all-reduce | flops 1536 | bytes 12288 | tf_op jit(solution)/shard_map/psum | solution.py:129
  379.7 1.8 convert_element_type.106
  381.5 1.6 convert_element_type.108
  383.1 188.3 %reduce-scatter.10.cloned.1.call-done = f32[64,3072]{1,0:T(8,128)} async-done(((f32[2048,3072]{1,0:T(8,128)}), f32[64,3072]{1,0:T(8,128)}) %reduce-scatter.10.cloned.1.call-update) | async-done | bytes 786448
  571.4 2.0 slice_bitcast_fusion
  (73 shorter events, 12.7 us)
Async XLA Ops:
  7.2 1.0 copy-start
  7.2 23.8 %copy-start.9 = (bf16[8,64,64]{2,1,0:T(8,128)(2,1)S(1)}, bf16[8,64,64]{2,1,0:T(8,128)(2,1)}, u32[]{:S(2)}) copy-start(bf16[8,64,64]{2,1,0:T(8,128)(2,1)} %param.12) | copy-start | bytes 196612
  7.2 62.2 %all-gather.3.cloned.1.call-start = ((), (), s32[]{:S(2)}) async-start(), calls=%async_computation.7 | async-start | bytes 2621440 | tf_op jit(solution)/shard_map/all_gather | solution.py:41
  10.0 36.3 %copy-start.2 = (bf16[512,512]{1,0:T(8,128)(2,1)S(1)}, bf16[512,512]{1,0:T(8,128)(2,1)}, u32[]{:S(2)}) copy-start(bf16[512,512]{1,0:T(8,128)(2,1)} %param.10) | copy-start | bytes 1572868
  10.0 36.3 %copy-start.10 = (f32[512]{0:T(512)S(1)}, f32[512]{0:T(512)}, u32[]{:S(2)}) copy-start(f32[512]{0:T(512)} %param.13) | copy-start | bytes 6148
  10.0 36.3 %copy-start.11 = (f32[512]{0:T(512)S(1)}, f32[512]{0:T(512)}, u32[]{:S(2)}) copy-start(f32[512]{0:T(512)} %param.14) | copy-start | bytes 6148
  31.0 15.2 %copy-start.3 = (bf16[64,8,512]{2,0,1:T(8,128)(2,1)}, bf16[64,8,512]{2,0,1:T(8,128)(2,1)S(1)}, u32[]{:S(2)}) copy-start(bf16[64,8,512]{2,0,1:T(8,128)(2,1)S(1)} %all_to_all.49) | copy-start | bytes 1572868
  31.6 39.8 %copy-start.15 = (f32[2048]{0:T(1024)S(1)}, f32[2048]{0:T(1024)}, u32[]{:S(2)}) copy-start(f32[2048]{0:T(1024)} %param.15) | copy-start | bytes 24580
  47.5 49.6 %all-gather.5.cloned.1.call-start = ((), (), s32[]{:S(2)}) async-start(), calls=%async_computation.9 | async-start | bytes 2621440 | tf_op jit(solution)/shard_map/all_gather | solution.py:60
  48.3 115.4 %reduce-scatter.8.cloned.1.call-start = ((), (), s32[]{:S(2)}) async-start(), calls=%async_computation.10 | async-start | bytes 5242880 | tf_op jit(solution)/shard_map/reduce_scatter | solution.py:88
  71.5 6.7 %copy-start.8 = (bf16[512,2048]{1,0:T(8,128)(2,1)S(1)}, bf16[512,2048]{1,0:T(8,128)(2,1)}, u32[]{:S(2)}) copy-start(bf16[512,2048]{1,0:T(8,128)(2,1)} %all-gather.3.cloned.1.call-done) | copy-start | bytes 6291460
  71.5 6.7 %copy-start.16 = (bf16[2048,1024]{1,0:T(8,128)(2,1)S(1)}, bf16[2048,1024]{1,0:T(8,128)(2,1)}, u32[]{:S(2)}) copy-start(bf16[2048,1024]{1,0:T(8,128)(2,1)} %param.16) | copy-start | bytes 12582916
  97.1 8.3 %copy-start.17 = (bf16[2048,1024]{1,0:T(8,128)(2,1)S(1)}, bf16[2048,1024]{1,0:T(8,128)(2,1)}, u32[]{:S(2)}) copy-start(bf16[2048,1024]{1,0:T(8,128)(2,1)} %param.16) | copy-start | bytes 12582916
  105.4 2.4 copy-start.19
  105.4 2.4 copy-start.20
  105.4 2.9 copy-start.18
  112.7 91.4 %reduce-scatter.6.cloned.1.call-start = ((), (), s32[]{:S(2)}) async-start(), calls=%async_computation.8 | async-start | bytes 2621440 | tf_op jit(solution)/shard_map/reduce_scatter | solution.py:49
  119.3 44.4 %copy-start.1 = (bf16[512,512]{1,0:T(8,128)(2,1)S(1)}, bf16[512,512]{1,0:T(8,128)(2,1)}, u32[]{:S(2)}) copy-start(bf16[512,512]{1,0:T(8,128)(2,1)} %fusion.11) | copy-start | bytes 1572868
  210.1 20.6 %all-to-all-start.2 = ((bf16[2,256,512]{2,0,1:T(2,128)(2,1)}), bf16[2,256,512]{2,0,1:T(2,128)(2,1)S(1)}, u32[]{:S(2)}, u32[]{:S(2)}) async-start(bf16[2,256,512]{2,0,1:T(2,128)(2,1)} %copy.33), calls=%async_computation.4 | async-start | bytes 1048576 | tf_op jit(solution)/shard_map/all_to_all | solution.py:103
  232.7 15.4 %all-to-all-start.3 = ((bf16[64,8,512]{2,1,0:T(8,128)(2,1)}), bf16[64,8,512]{2,1,0:T(8,128)(2,1)S(1)}, u32[]{:S(2)}, u32[]{:S(2)}) async-start(bf16[64,8,512]{2,1,0:T(8,128)(2,1)} %copy.36), calls=%async_computation.5 | async-start | bytes 1048576 | tf_op jit(solution)/shard_map/all_to_all | solution.py:116
  237.0 7.9 %copy-start.4 = (bf16[64,8,512]{2,0,1:T(8,128)(2,1)S(1)}, bf16[64,8,512]{2,0,1:T(8,128)(2,1)}, u32[]{:S(2)}) copy-start(bf16[64,8,512]{2,0,1:T(8,128)(2,1)} %copy-done.3) | copy-start | bytes 1572868
  237.0 142.6 %all-reduce.4.cloned.1.call-start = ((), (), s32[]{:S(2)}) async-start(), calls=%async_computation.12 | async-start | bytes 786432 | tf_op jit(solution)/shard_map/psum | solution.py:126
  248.0 19.5 %copy-start.6 = (bf16[64,8,512]{2,1,0:T(8,128)(2,1)}, bf16[64,8,512]{2,1,0:T(8,128)(2,1)S(1)}, u32[]{:S(2)}) copy-start(bf16[64,8,512]{2,1,0:T(8,128)(2,1)S(1)} %all-to-all-done.3) | copy-start | bytes 1572868
  249.1 322.3 %reduce-scatter.10.cloned.1.call-start = ((), (), s32[]{:S(2)}) async-start(), calls=%async_computation.11 | async-start | bytes 25952256
  292.3 0.7 copy-start.12
  292.3 0.7 copy-start.13
  292.3 0.7 copy-start.14
  292.3 85.8 %copy-start.7 = (bf16[64,8,512]{2,1,0:T(8,128)(2,1)S(1)}, bf16[64,8,512]{2,1,0:T(8,128)(2,1)}, u32[]{:S(2)}) copy-start(bf16[64,8,512]{2,1,0:T(8,128)(2,1)} %copy-done.6) | copy-start | bytes 1572868
  292.3 86.1 %copy-start.5 = (f32[512,512]{1,0:T(8,128)S(1)}, f32[512,512]{1,0:T(8,128)}, u32[]{:S(2)}) copy-start(f32[512,512]{1,0:T(8,128)} %get-tuple-element.39) | copy-start | bytes 3145732
Sparse Core Ops, SparseCore 0:
  47.6 21.6 all-gather.2
  71.1 26.0 all-gather.4
  112.9 50.8 reduce-scatter.7
  166.4 37.7 reduce-scatter.5
  249.2 38.3 all-reduce.3
  292.5 278.8 reduce-scatter.9
where the time goes:
time: 583 us; the launch traced here: 580 us
  waiting for transfers between devices  295 us (51%)
  blocking collectives  131 us (22%)
  matrix products  59.4 us (10%)
  local copies, waits for them, and re-layouts  33.5 us (6%)
  other arithmetic  33.1 us (6%)
  between operations  14.4 us (2%)
  starting transfers between devices  14.3 us (2%)
    unnamed x7, waiting for transfers between devices  189 us
    psum x1, blocking collectives, on_device(): lax.psum((scale_local, shift_local, gain_local), 'seq')  85.1 us
    reduce_scatter x1, waiting for transfers between devices, on_device(): lax.psum_scatter(total + lax.dot_general(w_up, up_back, contract, preferr...  36 us
    reduce_scatter x1, waiting for transfers between devices, on_device(): lax.psum_scatter(lax.dot_general(w_down, hidden, (((0,), (1,)), ((), ()))...  27.5 us
    unnamed x43, local copies, waits for them, and re-layouts  26.9 us
    all_gather x1, waiting for transfers between devices, on_device(): whole = lax.all_gather(mixed, 'chan', axis=1, tiled=True)  20.9 us
    all_to_all x1, blocking collectives, on_device(): lax.all_to_all(first_local, 'seq', split_axis=1, concat_axis=0, tiled=True)  20.4 us
    concatenate x1, other arithmetic, on_device(): jnp.concatenate([jnp.concatenate([gate_term, up_term], axis=1), lax.dot_g...  18.4 us
  transfers between devices with their start and end apart: 8, of which 7 were waited for; matrix products, arithmetic and copies ran while one was open for 16% of the time, Pallas kernels for 0%

commit v1 on v0

--- a/solution.py
+++ b/solution.py
@@ -1,7 +1,205 @@
+import functools
+
 import jax
 import jax.numpy as jnp
 from jax import lax
+from jax.experimental import pallas as pl
+from jax.experimental.pallas import tpu as pltpu
 from jax.sharding import PartitionSpec as P
+
+MESH = pl.DeviceIdType.MESH
+PARTS = 32
+SLAB = 16
+ROWS = 512
+PIECES = 4
+PIECE = ROWS // PIECES
+
+
+def interleaved(low, high):
+    pair = [part.reshape(PARTS, 8, part.shape[1]) for part in (low, high)]
+    return jnp.stack(pair, axis=1).reshape(ROWS, low.shape[1])
+
+
+def dot(a, b):
+    return jnp.dot(a, b, preferred_element_type=jnp.float32)
+
+
+def place():
+    return lax.axis_index("seq"), lax.axis_index("chan")
+
+
+def greet():
+    s, c = place()
+    barrier = pltpu.get_barrier_semaphore()
+
+    def greet_seq(step, carry):
+        target = (lax.rem(s + step, PARTS), c)
+        pl.semaphore_signal(barrier, inc=1, device_id=target, device_id_type=MESH)
+        return carry
+
+    lax.fori_loop(1, PARTS, greet_seq, 0)
+    for step in range(1, 4):
+        target = (s, lax.rem(c + step, 4))
+        pl.semaphore_signal(barrier, inc=1, device_id=target, device_id_type=MESH)
+    pl.semaphore_wait(barrier, PARTS - 1 + 3)
+
+
+def slab(index):
+    return pl.ds(pl.multiple_of(index * SLAB, SLAB), SLAB)
+
+
+def swap_start(src, dst, send, recv):
+    s, c = place()
+
+    def one(step, carry):
+        target = lax.rem(s + step, PARTS)
+        pltpu.make_async_remote_copy(
+            src_ref=src.at[slab(target)],
+            dst_ref=dst.at[slab(s)],
+            send_sem=send,
+            recv_sem=recv,
+            device_id=(target, c),
+            device_id_type=MESH,
+        ).start()
+        return carry
+
+    lax.fori_loop(1, PARTS, one, 0)
+    dst[slab(s), :] = src[slab(s), :]
+
+
+def swap_wait(src, dst, send, recv):
+    s, c = place()
+    most = pl.ds(0, ROWS - SLAB)
+    pltpu.make_async_remote_copy(
+        src_ref=src.at[most],
+        dst_ref=dst.at[most],
+        send_sem=send,
+        recv_sem=recv,
+        device_id=(lax.rem(s + 1, PARTS), c),
+        device_id_type=MESH,
+    ).wait()
+
+
+def chan_copy(buf, owner, piece, lane, send, recv, target):
+    part = buf.at[owner, pl.ds(piece * PIECE, PIECE)]
+    return pltpu.make_async_remote_copy(
+        src_ref=part,
+        dst_ref=part,
+        send_sem=send.at[lane, piece],
+        recv_sem=recv.at[lane, piece],
+        device_id=target,
+        device_id_type=MESH,
+    )
+
+
+def gather_copy(buf, piece, lane, send, recv):
+    s, c = place()
+    across, beside = lax.rem(c + 2, 4), c + 1 - 2 * lax.rem(c, 2)
+    owner = across if lane == 2 else c
+    target = across if lane == 0 else beside
+    return chan_copy(buf, owner, piece, lane, send, recv, (s, target))
+
+
+def gather_start(buf, piece, send, recv):
+    gather_copy(buf, piece, 0, send, recv).start()
+    gather_copy(buf, piece, 1, send, recv).start()
+
+
+def gather_forward(buf, piece, send, recv):
+    gather_copy(buf, piece, 0, send, recv).wait_recv()
+    gather_copy(buf, piece, 2, send, recv).start()
+
+
+def gather_finish(buf, piece, send, recv):
+    gather_copy(buf, piece, 1, send, recv).wait()
+    gather_copy(buf, piece, 2, send, recv).wait()
+    gather_copy(buf, piece, 0, send, recv).wait_send()
+
+
+def spread_two(f2):
+    shape = (ROWS, ROWS)
+    row = lax.broadcasted_iota(jnp.int32, shape, 0)
+    col = lax.broadcasted_iota(jnp.int32, shape, 1)
+    same = jnp.bitwise_and(row, 7) == jnp.bitwise_and(col, 7)
+    order = col == jnp.bitwise_and(row, 7) * 64 + lax.shift_right_logical(row, 3)
+    order = order.astype(jnp.float32).astype(jnp.bfloat16)
+    short = (64, ROWS)
+    row = lax.broadcasted_iota(jnp.int32, short, 0)
+    col = lax.broadcasted_iota(jnp.int32, short, 1)
+    widen = (row == lax.shift_right_logical(col, 3)).astype(jnp.float32).astype(jnp.bfloat16)
+    wide = dot(f2.reshape(ROWS, 64), widen).astype(jnp.bfloat16)
+    return jnp.where(same, dot(order, wide), 0.0).astype(jnp.bfloat16)
+
+
+def mixer(
+    x, og, f1, f2, scale, shift,
+    wm, cot, first_cols, seqmix,
+    src, xin, big_two, swap_send, swap_recv, gs, gr, hs, hr,
+):
+    s, c = place()
+    lane = pl.ds(0, 256)
+    lane2 = pl.ds(256, 256)
+    f32 = jnp.float32
+    cot[c] = interleaved(og[lane].astype(f32), og[lane2].astype(f32)).astype(jnp.bfloat16)
+    src[0] = interleaved(dot(f1[0], x[lane]), dot(f1[1], x[lane2])).astype(jnp.bfloat16)
+    greet()
+    swap_start(src.at[0], first_cols, swap_send.at[0], swap_recv.at[0])
+    for piece in range(PIECES):
+        gather_start(cot, piece, hs, hr)
+    xin[...] = interleaved(x[lane].astype(f32), x[lane2].astype(f32)).astype(jnp.bfloat16)
+    big_two[...] = spread_two(f2[...])
+    swap_wait(src.at[0], first_cols, swap_send.at[0], swap_recv.at[0])
+    src[1] = dot(big_two[...], first_cols[...]).astype(jnp.bfloat16)
+    swap_start(src.at[1], seqmix, swap_send.at[1], swap_recv.at[1])
+    for piece in range(PIECES):
+        gather_forward(cot, piece, hs, hr)
+    swap_wait(src.at[1], seqmix, swap_send.at[1], swap_recv.at[1])
+    for piece in range(PIECES):
+        rows = pl.ds(piece * PIECE, PIECE)
+        xf = xin[rows].astype(f32)
+        opening = jax.nn.sigmoid(xf * scale[...] + shift[...])
+        wm[c, rows] = (xf + opening * seqmix[rows].astype(f32)).astype(jnp.bfloat16)
+        gather_start(wm, piece, gs, gr)
+    for piece in range(PIECES):
+        gather_finish(cot, piece, hs, hr)
+    for piece in range(PIECES):
+        gather_forward(wm, piece, gs, gr)
+    for piece in range(PIECES):
+        gather_finish(wm, piece, gs, gr)
+
+
+def call_mixer(layer_in, out_grad, factor_one, factor_two, scale, shift):
+    vmem = pl.BlockSpec(memory_space=pltpu.VMEM)
+    bf = jnp.bfloat16
+    square = jax.ShapeDtypeStruct((ROWS, ROWS), bf)
+    whole = jax.ShapeDtypeStruct((4, ROWS, ROWS), bf)
+    dma = pltpu.SemaphoreType.DMA
+    return pl.pallas_call(
+        mixer,
+        out_shape=(whole, whole, square, square),
+        in_specs=[vmem] * 6,
+        out_specs=(vmem,) * 4,
+        scratch_shapes=[
+            pltpu.VMEM((2, ROWS, ROWS), bf),
+            pltpu.VMEM((ROWS, ROWS), bf),
+            pltpu.VMEM((ROWS, ROWS), bf),
+            dma((2,)),
+            dma((2,)),
+            dma((3, PIECES)),
+            dma((3, PIECES)),
+            dma((3, PIECES)),
+            dma((3, PIECES)),
+        ],
+        compiler_params=pltpu.CompilerParams(
+            collective_id=0, has_side_effects=True, vmem_limit_bytes=48 << 20
+        ),
+        name="mixer",
+    )(layer_in, out_grad, factor_one, factor_two, scale.reshape(1, -1), shift.reshape(1, -1))
+
+
+def plain(array):
+    width = array.shape[-1]
+    return array.reshape(PARTS, 2, 8, width).swapaxes(0, 1).reshape(ROWS, width)
 
 
 def on_device(
@@ -24,21 +222,17 @@
     dims_first = (((0,), (0,)), ((), ()))
     in_float = layer_in.astype(jnp.float32)
     in_blocks = layer_in.reshape(block_count, block, width)
-    first_local = jnp.einsum(
-        "pkq,pqc->pkc", factor_one, in_blocks, preferred_element_type=jnp.float32
-    ).astype(jnp.bfloat16)
-    first_cols = lax.all_to_all(first_local, "seq", split_axis=1, concat_axis=0, tiled=True)
-    second_cols = jnp.einsum(
-        "qjp,pqc->jqc", factor_two, first_cols, preferred_element_type=jnp.float32
-    ).astype(jnp.bfloat16)
-    second_rows = lax.all_to_all(
-        second_cols, "seq", split_axis=0, concat_axis=1, tiled=True
-    ).reshape(rows, width)
-    seqmix = second_rows.astype(jnp.float32)
+    whole, cot_whole, first_cols, second_rows = call_mixer(
+        layer_in, out_grad, factor_one, factor_two, gate_scale, gate_shift
+    )
+    own = lax.axis_index("chan")
+    first_cols = first_cols.reshape(64, 8, width)
+    mixed_float = plain(lax.dynamic_index_in_dim(whole, own, 0, False)).astype(jnp.float32)
+    whole, cot_whole = [
+        jnp.concatenate([plain(part[k]) for k in range(4)], axis=1) for part in (whole, cot_whole)
+    ]
+    seqmix = plain(second_rows).astype(jnp.float32)
     opening = jax.nn.sigmoid(in_float * gate_scale + gate_shift)
-    mixed = (in_float + opening * seqmix).astype(jnp.bfloat16)
-    mixed_float = mixed.astype(jnp.float32)
-    whole = lax.all_gather(mixed, "chan", axis=1, tiled=True)
     whole_float = whole.astype(jnp.float32)
     inv_rms = lax.rsqrt(jnp.mean(whole_float * whole_float, axis=1, keepdims=True) + 1e-05)
     normed = (whole_float * inv_rms * norm_gain).astype(jnp.bfloat16)
@@ -57,7 +251,6 @@
     layer_out = (mixed_float + mlp_cols.T).astype(jnp.bfloat16)
     offset = lax.axis_index("chan") * width
     gain_own = lax.dynamic_slice_in_dim(norm_gain, offset, width, 0)
-    cot_whole = lax.all_gather(out_grad, "chan", axis=1, tiled=True)
     hidden_grad = lax.dot_general(
         cot_whole, w_down, (((1,), (1,)), ((), ())), preferred_element_type=jnp.float32
     )
@@ -75,11 +268,11 @@
                 lax.dot_general(cot_whole, hidden, dims_first, preferred_element_type=jnp.float32),
             ],
             axis=1,
-        ),
+        ).astype(jnp.bfloat16),
         "seq",
         scatter_dimension=0,
         tiled=True,
-    )
+    ).astype(jnp.float32)
     gate_part = joint_part[:, :hidden_width]
     up_part = joint_part[:, hidden_width : 2 * hidden_width]
     down_part = joint_part[:, 2 * hidden_width :]

time: 583 us -> 449 us (0.77)
  waiting for transfers between devices: 295 us -> 173 us
  Pallas kernels: 0 us -> 47.1 us
  blocking collectives: 131 us -> 92 us
  matrix products: 59.4 us -> 43.4 us
  other arithmetic: 33.1 us -> 22.9 us
  local copies, waits for them, and re-layouts: 33.5 us -> 39.4 us
    unnamed x7 -> x5, waiting for transfers between devices: 189 us -> 102 us
    pallas_call x0 -> x1, Pallas kernels: none -> 47.1 us  [call_mixer(): pl.pallas_call(mixer, out_shape=(whole, whole, square, square), in_specs=...]
    all_gather x2 -> x0, waiting for transfers between devices: 36.1 us -> none  [the longest x1 20.9 us: on_device(): whole = lax.all_gather(mixed, 'chan', axis=1, tiled=True)]
    all_to_all x2 -> x0, blocking collectives: 34.9 us -> none  [the longest x1 20.4 us: on_device(): lax.all_to_all(first_local, 'seq', split_axis=1, concat_axis=0, tiled=True)]
    concatenate x1, other arithmetic: 18.4 us -> 11.4 us  [on_device(): jnp.concatenate([jnp.concatenate([gate_term, up_term], axis=1), lax.dot_g...]
    unnamed x43 -> x65, local copies, waits for them, and re-layouts: 26.9 us -> 31.8 us
  transfers between devices with their start and end apart: 8 -> 6, of which waited for: 7 -> 5; matrix products, arithmetic and copies ran while one was open for 16% -> 14% of each run, Pallas kernels for 0% -> 0%
where the time goes in v1:
time: 449 us; the launch traced here: 447 us
  waiting for transfers between devices  173 us (39%)
  blocking collectives  92 us (20%)
  Pallas kernels  47.1 us (10%)
  matrix products  43.4 us (10%)
  local copies, waits for them, and re-layouts  39.4 us (9%)
  other arithmetic  22.9 us (5%)
  between operations  15.6 us (3%)
  starting transfers between devices  13.9 us (3%)
    unnamed x5, waiting for transfers between devices  102 us
    psum x1, blocking collectives, on_device(): lax.psum((scale_local, shift_local, gain_local), 'seq')  81.9 us
    pallas_call x1, Pallas kernels, call_mixer(): pl.pallas_call(mixer, out_shape=(whole, whole, square, square), in_specs=...  47.1 us
    reduce_scatter x1, waiting for transfers between devices, on_device(): lax.psum_scatter(total + lax.dot_general(w_up, up_back, contract, preferr...  34 us
    unnamed x65, local copies, waits for them, and re-layouts  31.8 us
    reduce_scatter x1, waiting for transfers between devices, on_device(): lax.psum_scatter(lax.dot_general(w_down, hidden, (((0,), (1,)), ((), ()))...  28.9 us
    concatenate x1, other arithmetic, on_device(): jnp.concatenate([jnp.concatenate([gate_term, up_term], axis=1), lax.dot_g...  11.4 us
    psum x1, blocking collectives, on_device(): row_dots = lax.psum(row_local, 'chan')  10.1 us
  transfers between devices with their start and end apart: 6, of which 5 were waited for; matrix products, arithmetic and copies ran while one was open for 14% of the time, Pallas kernels for 0%

profile of v1, /device:TPU:16, one launch (start us, length us, event | category | flops | bytes accessed | tf_op | source)
XLA Modules:
  0.0 447.0 jit_solution(15869282672763275082)
XLA Ops:
  13.4 47.1 %mixer.1 = (bf16[4,512,512]{2,1,0:T(8,128)(2,1)S(1)}, bf16[4,512,512]{2,1,0:T(8,128)(2,1)}, bf16[512,512]{1,0:T(8,128)(2,1)S(1)}, bf16[512,512]{1,0:T(8,128)(2,1)S(1)}) custom-call(bf16[512,512]{1,0:T(8,128)(2,1)S(1)} %copy-done, bf16[512,512]{1,0:T(8,128)(2,1)S(1)} %copy-done.2, bf16[2,256,256]{2,1,0:T(8,128)(2,1)S(1)} %copy-done.4, ...), custom_call_target="tpu_custom_call" | custom-call | tf_op jit(solution)/shard_map/mixer/pallas_call | solution.py:177
  60.5 1.9 fusion.43
  63.1 2.0 copy-done.24
  65.2 2.4 fusion.38
  67.6 2.4 fusion.36
  70.2 2.7 copy-done.26
  72.9 4.1 multiply_convert_fusion
  77.1 2.4 fusion.46
  79.5 4.4 add_bitcast_fusion
  85.1 5.9 %fusion.3 = bf16[2048,512]{0,1:T(8,128)(2,1)} fusion(bf16[512,1024]{1,0:T(8,128)(2,1)S(1)} %copy-done.29, bf16[1024,2048]{1,0:T(8,128)(2,1)} %param.18), kind=kOutput, calls=%fused_computation.11 | convolution fusion | flops 2148532224 | bytes 7340032 | tf_op jit(solution)/shard_map/dot_general | solution.py:244
  92.6 6.5 %convolution_convert_fusion.1 = bf16[2048,1024]{0,1:T(8,128)(2,1)} fusion(bf16[512,1024]{1,0:T(8,128)(2,1)} %copy-done.28, f32[2048]{0:T(1024)S(1)} %copy-done.23, f32[512]{0:T(512)S(1)} %add_rsqrt_fusion, bf16[512,512]{1,0:T(8,128)(2,1)S(1)} %bitcast.144, bf16[512,512]{1,0:T(8,128)(2,1)} %bitcast.149, bf16[512,512]{1,0:T(8,128)(2,1)} %bitcast.154, ...), kind=kOutput, calls=%fused_computation.8 | convolution fusion | flops 2161115136 | bytes 7350272 | tf_op jit(solution)/shard_map/dot_general | solution.py:263
  99.1 34.0 %reduce-scatter.8.cloned.1.call-done = f32[512,512]{0,1:T(8,128)} async-done(((f32[2048,512]{0,1:T(8,128)}), f32[512,512]{0,1:T(8,128)}) %reduce-scatter.8.cloned.1.call-update) | async-done | bytes 1048592 | tf_op jit(solution)/shard_map/reduce_scatter | solution.py:281
  133.1 1.6 fusion.19
  134.7 10.1 %psum.42 = f32[512]{0:T(512)S(1)} all-reduce(f32[512]{0:T(512)S(1)} %get-tuple-element.49), channel_id=1, replica_groups=mesh['seq'=32,'chan'=4] {'chan'}, use_global_device_ids=true, to_apply=%region_4.5 | all-reduce | flops 512 | bytes 4096 | tf_op jit(solution)/shard_map/psum | solution.py:288
  144.8 28.9 %reduce-scatter.6.cloned.1.call-done = bf16[512,512]{0,1:T(8,128)(2,1)} async-done(((bf16[2048,512]{0,1:T(8,128)(2,1)}), bf16[512,512]{0,1:T(8,128)(2,1)}) %reduce-scatter.6.cloned.1.call-update) | async-done | bytes 524304 | tf_op jit(solution)/shard_map/reduce_scatter | solution.py:243
  173.7 4.2 fusion.40
  178.2 1.3 copy.58
  179.5 9.1 %all-to-all-start = ((bf16[2,256,512]{2,0,1:T(2,128)(2,1)}), bf16[2,256,512]{2,0,1:T(2,128)(2,1)}, u32[]{:S(2)}, u32[]{:S(2)}) async-start(bf16[2,256,512]{2,0,1:T(2,128)(2,1)} %copy.58), calls=%async_computation.2 | async-start | bytes 1048576 | tf_op jit(solution)/shard_map/all_to_all | solution.py:296
  188.7 6.3 %convolution_convert_fusion.2 = bf16[2048,1024]{0,1:T(8,128)(2,1)} fusion(bf16[512,1024]{1,0:T(8,128)(2,1)} %copy-done.27, f32[2048]{0:T(1024)S(1)} %copy-done.23, f32[512]{0:T(512)S(1)} %add_rsqrt_fusion, bf16[512,512]{1,0:T(8,128)(2,1)S(1)} %bitcast.145, bf16[512,512]{1,0:T(8,128)(2,1)} %bitcast.150, bf16[512,512]{1,0:T(8,128)(2,1)} %bitcast.155, ...), kind=kOutput, calls=%fused_computation.9 | convolution fusion | flops 2161115136 | bytes 7350272 | tf_op jit(solution)/shard_map/dot_general | solution.py:262
  194.9 5.3 %all-to-all-done = bf16[2,256,512]{2,0,1:T(2,128)(2,1)} async-done(((bf16[2,256,512]{2,0,1:T(2,128)(2,1)}), bf16[2,256,512]{2,0,1:T(2,128)(2,1)}, u32[]{:S(2)}, u32[]{:S(2)}) %all-to-all-start) | async-done | bytes 524320 | tf_op jit(solution)/shard_map/all_to_all | solution.py:296
  200.2 1.4 copy.83
  203.3 4.2 all-to-all-start.1
  207.8 6.2 %convolution_convert_fusion = bf16[2048,1024]{0,1:T(8,128)(2,1)} fusion(bf16[512,1024]{1,0:T(8,128)(2,1)} %get-tuple-element.61, bf16[512,512]{1,0:T(8,128)(2,1)} %bitcast.174, bf16[512,512]{1,0:T(8,128)(2,1)} %bitcast.176, bf16[512,512]{1,0:T(8,128)(2,1)} %bitcast.178, bf16[512,512]{1,0:T(8,128)(2,1)} %bitcast.180), kind=kOutput, calls=%fused_computation.7 | convolution fusion | flops 2157969408 | bytes 7340032 | tf_op jit(solution)/shard_map/dot_general | solution.py:268
  215.0 3.0 all-to-all-done.1
  219.2 11.4 %pad_maximum_fusion = bf16[2048,3072]{0,1:T(8,128)(2,1)} fusion(bf16[2048,1024]{0,1:T(8,128)(2,1)} %convolution_convert_fusion, bf16[2048,1024]{0,1:T(8,128)(2,1)} %convolution_convert_fusion.1, bf16[2048,1024]{0,1:T(8,128)(2,1)} %convolution_convert_fusion.2), kind=kLoop, calls=%fused_computation | loop fusion | flops 37748736 | bytes 25165824 | tf_op jit(solution)/shard_map/concatenate | solution.py:265
  230.6 16.6 %copy.70 = bf16[2048,3072]{1,0:T(8,128)(2,1)} copy(bf16[2048,3072]{0,1:T(8,128)(2,1)} %pad_maximum_fusion) | data formatting | bytes 25165824
  247.3 81.9 %all-reduce = (f32[512]{0:T(512)}, f32[512]{0:T(512)}, f32[512]{0:T(512)}) all-reduce(f32[512]{0:T(512)S(1)} %get-tuple-element.51, f32[512]{0:T(512)S(1)} %get-tuple-element.50, f32[512]{0:T(512)S(1)} %get-tuple-element.48), channel_id=1, replica_groups=mesh['seq'=32,'chan'=4] {'seq'}, use_global_device_ids=true, to_apply=%region_8.9 | all-reduce | flops 1536 | bytes 12288 | tf_op jit(solution)/shard_map/psum | solution.py:322
  329.5 1.2 fusion.11
  330.7 1.8 convert_element_type.106
  332.5 1.6 convert_element_type.108
  334.1 101.5 %reduce-scatter.10.cloned.1.call-done = bf16[64,3072]{1,0:T(8,128)(2,1)} async-done(((bf16[2048,3072]{1,0:T(8,128)(2,1)}), bf16[64,3072]{1,0:T(8,128)(2,1)}) %reduce-scatter.10.cloned.1.call-update) | async-done | bytes 393232
  435.6 1.4 copy.71
  (95 shorter events, 16.5 us)
Async XLA Ops:
  8.0 125.1 %reduce-scatter.8.cloned.1.call-start = ((), (), s32[]{:S(2)}) async-start(), calls=%async_computation.6 | async-start | bytes 5242880 | tf_op jit(solution)/shard_map/reduce_scatter | solution.py:281
  8.1 1.0 copy-start
  9.1 1.0 copy-start.2
  10.1 0.9 copy-start.4
  62.4 2.8 copy-start.24
  62.5 5.0 %copy-start.14 = (bf16[32,2,8,512]{3,2,0,1:T(8,128)(2,1)}, bf16[32,2,8,512]{3,2,0,1:T(8,128)(2,1)S(1)}, u32[]{:S(2)}) copy-start(bf16[32,2,8,512]{3,2,0,1:T(8,128)(2,1)S(1)} %copy.51) | copy-start | bytes 1572868
  62.5 5.0 %copy-start.15 = (bf16[32,2,8,512]{3,2,0,1:T(8,128)(2,1)}, bf16[32,2,8,512]{3,2,0,1:T(8,128)(2,1)S(1)}, u32[]{:S(2)}) copy-start(bf16[32,2,8,512]{3,2,0,1:T(8,128)(2,1)S(1)} %copy.50) | copy-start | bytes 1572868
  62.6 5.0 %copy-start.16 = (bf16[32,2,8,512]{3,2,0,1:T(8,128)(2,1)}, bf16[32,2,8,512]{3,2,0,1:T(8,128)(2,1)S(1)}, u32[]{:S(2)}) copy-start(bf16[32,2,8,512]{3,2,0,1:T(8,128)(2,1)S(1)} %copy.49) | copy-start | bytes 1572868
  65.2 2.4 copy-start.25
  70.0 2.9 copy-start.26
  70.0 7.0 %copy-start.19 = (bf16[32,2,8,512]{3,2,0,1:T(8,128)(2,1)}, bf16[32,2,8,512]{3,2,0,1:T(8,128)(2,1)S(1)}, u32[]{:S(2)}) copy-start(bf16[32,2,8,512]{3,2,0,1:T(8,128)(2,1)S(1)} %copy.56) | copy-start | bytes 1572868
  70.1 7.0 %copy-start.20 = (bf16[32,2,8,512]{3,2,0,1:T(8,128)(2,1)}, bf16[32,2,8,512]{3,2,0,1:T(8,128)(2,1)S(1)}, u32[]{:S(2)}) copy-start(bf16[32,2,8,512]{3,2,0,1:T(8,128)(2,1)S(1)} %copy.55) | copy-start | bytes 1572868
  70.1 6.9 %copy-start.21 = (bf16[32,2,8,512]{3,2,0,1:T(8,128)(2,1)}, bf16[32,2,8,512]{3,2,0,1:T(8,128)(2,1)S(1)}, u32[]{:S(2)}) copy-start(bf16[32,2,8,512]{3,2,0,1:T(8,128)(2,1)S(1)} %copy.54) | copy-start | bytes 1572868
  70.2 6.9 %copy-start.22 = (bf16[32,2,8,512]{3,2,0,1:T(8,128)(2,1)}, bf16[32,2,8,512]{3,2,0,1:T(8,128)(2,1)S(1)}, u32[]{:S(2)}) copy-start(bf16[32,2,8,512]{3,2,0,1:T(8,128)(2,1)S(1)} %copy.53) | copy-start | bytes 1572868
  77.1 2.4 copy-start.27
  77.1 2.4 copy-start.28
  83.9 1.2 copy-start.29
  83.9 89.8 %reduce-scatter.6.cloned.1.call-start = ((), (), s32[]{:S(2)}) async-start(), calls=%async_computation.5 | async-start | bytes 2621440 | tf_op jit(solution)/shard_map/reduce_scatter | solution.py:243
  92.5 40.6 %copy-start.12 = (f32[2,32,8,512]{3,2,1,0:T(8,128)}, f32[2,32,8,512]{3,2,1,0:T(8,128)S(1)}, u32[]{:S(2)}) copy-start(f32[2,32,8,512]{3,2,1,0:T(8,128)S(1)} %copy.48) | copy-start | bytes 3145732
  92.6 81.1 %copy-start.1 = (bf16[512,512]{1,0:T(8,128)(2,1)S(1)}, bf16[512,512]{1,0:T(8,128)(2,1)}, u32[]{:S(2)}) copy-start(bf16[512,512]{1,0:T(8,128)(2,1)} %x.1) | copy-start | bytes 1572868
  92.6 81.1 %copy-start.3 = (bf16[512,512]{1,0:T(8,128)(2,1)S(1)}, bf16[512,512]{1,0:T(8,128)(2,1)}, u32[]{:S(2)}) copy-start(bf16[512,512]{1,0:T(8,128)(2,1)} %og.1) | copy-start | bytes 1572868
  92.6 81.1 %copy-start.9 = (f32[512]{0:T(512)S(1)}, f32[512]{0:T(512)}, u32[]{:S(2)}) copy-start(f32[512]{0:T(512)} %param.13) | copy-start | bytes 6148
  92.6 81.1 %copy-start.11 = (f32[512]{0:T(512)S(1)}, f32[512]{0:T(512)}, u32[]{:S(2)}) copy-start(f32[512]{0:T(512)} %param.14) | copy-start | bytes 6148
  179.5 20.7 %all-to-all-start = ((bf16[2,256,512]{2,0,1:T(2,128)(2,1)}), bf16[2,256,512]{2,0,1:T(2,128)(2,1)}, u32[]{:S(2)}, u32[]{:S(2)}) async-start(bf16[2,256,512]{2,0,1:T(2,128)(2,1)} %copy.58), calls=%async_computation.2 | async-start | bytes 1048576 | tf_op jit(solution)/shard_map/all_to_all | solution.py:296
  188.7 13.2 %copy-start.7 = (bf16[8,64,64]{2,1,0:T(8,128)(2,1)S(1)}, bf16[8,64,64]{2,1,0:T(8,128)(2,1)}, u32[]{:S(2)}) copy-start(bf16[8,64,64]{2,1,0:T(8,128)(2,1)} %f2.1) | copy-start | bytes 196612
  201.8 1.5 copy-start.17
  203.3 14.8 %all-to-all-start.1 = ((bf16[64,8,512]{2,1,0:T(8,128)(2,1)}), bf16[64,8,512]{2,1,0:T(8,128)(2,1)S(1)}, u32[]{:S(2)}, u32[]{:S(2)}) async-start(bf16[64,8,512]{2,1,0:T(8,128)(2,1)} %copy.61), calls=%async_computation.3 | async-start | bytes 1048576 | tf_op jit(solution)/shard_map/all_to_all | solution.py:309
  207.5 6.5 %copy-start.18 = (bf16[64,8,512]{2,0,1:T(8,128)(2,1)S(1)}, bf16[64,8,512]{2,0,1:T(8,128)(2,1)}, u32[]{:S(2)}) copy-start(bf16[64,8,512]{2,0,1:T(8,128)(2,1)} %copy-done.17) | copy-start | bytes 1572868
  207.5 123.2 %all-reduce.4.cloned.1.call-start = ((), (), s32[]{:S(2)}) async-start(), calls=%async_computation.8 | async-start | bytes 786432 | tf_op jit(solution)/shard_map/psum | solution.py:319
  219.1 216.5 %reduce-scatter.10.cloned.1.call-start = ((), (), s32[]{:S(2)}) async-start(), calls=%async_computation.7 | async-start | bytes 12976128
  247.2 81.9 %copy-start.5 = (bf16[2,256,256]{2,1,0:T(8,128)(2,1)S(1)}, bf16[2,256,256]{2,1,0:T(8,128)(2,1)}, u32[]{:S(2)}) copy-start(bf16[2,256,256]{2,1,0:T(8,128)(2,1)} %f1.1) | copy-start | bytes 786436
  247.2 82.2 %copy-start.13 = (f32[512,512]{1,0:T(8,128)S(1)}, f32[512,512]{1,0:T(8,128)}, u32[]{:S(2)}) copy-start(f32[512,512]{1,0:T(8,128)} %get-tuple-element.57) | copy-start | bytes 3145732
  (4 other events, 3.0 us)
Sparse Core Ops, SparseCore 0:
  84.0 49.0 reduce-scatter.7
  135.9 37.7 reduce-scatter.5
  219.2 37.6 all-reduce.3
Sparse Core Ops, SparseCore 1:
  247.4 188.2 reduce-scatter.9

commit v2 on v1

v2 whole, which is shorter than its diff:
```python
import jax
import jax.numpy as jnp
from jax import lax
from jax.experimental import pallas as pl
from jax.experimental.pallas import tpu as pltpu
from jax.sharding import PartitionSpec as P

MESH = pl.DeviceIdType.MESH
PARTS = 32
SLAB = 16
ROWS = 512
PIECES = 4
PIECE = ROWS // PIECES
BLOCK = 512
HIDDEN = 1024
UNITS = 6
SLOTS = 4
SHARE = 64
VMEM_LIMIT = 67000000


def interleaved(low, high):
    rows, width = low.shape
    pair = [part.reshape(rows // 8, 8, width) for part in (low, high)]
    return jnp.stack(pair, axis=1).reshape(2 * rows, width)


def inside(ref, piece):
    return interleaved(
        *[full(ref[pl.ds(k * 256 + piece * PIECE // 2, PIECE // 2)]) for k in range(2)]
    )


def deal(whole):
    parts = whole.reshape(PARTS, 2, 8, whole.shape[1])
    return [parts[:, k].reshape(ROWS // 2, whole.shape[1]) for k in range(2)]


def dot(a, b):
    return jnp.dot(a, b, preferred_element_type=jnp.float32)


def dot_rows(a, b):
    return lax.dot_general(a, b, (((1,), (1,)), ((), ())), preferred_element_type=jnp.float32)


def half(values):
    return values.astype(jnp.bfloat16)


def full(values):
    return values.astype(jnp.float32)


def place():
    return lax.axis_index("seq"), lax.axis_index("chan")


def greet():
    s, c = place()
    barrier = pltpu.get_barrier_semaphore()

    def greet_seq(step, carry):
        target = (lax.rem(s + step, PARTS), c)
        pl.semaphore_signal(barrier, inc=1, device_id=target, device_id_type=MESH)
        return carry

    lax.fori_loop(1, PARTS, greet_seq, 0)
    for step in range(1, 4):
        target = (s, lax.rem(c + step, 4))
        pl.semaphore_signal(barrier, inc=1, device_id=target, device_id_type=MESH)
    pl.semaphore_wait(barrier, PARTS - 1 + 3)


def slab(index):
    return pl.ds(pl.multiple_of(index * SLAB, SLAB), SLAB)


def swap_start(src, dst, send, recv):
    s, c = place()

    def one(step, carry):
        target = lax.rem(s + step, PARTS)
        pltpu.make_async_remote_copy(
            src_ref=src.at[slab(target)],
            dst_ref=dst.at[slab(s)],
            send_sem=send,
            recv_sem=recv,
            device_id=(target, c),
            device_id_type=MESH,
        ).start()
        return carry

    lax.fori_loop(1, PARTS, one, 0)
    dst[slab(s), :] = src[slab(s), :]


def swap_wait(src, dst, send, recv):
    s, c = place()
    most = pl.ds(0, ROWS - SLAB)
    pltpu.make_async_remote_copy(
        src_ref=src.at[most],
        dst_ref=dst.at[most],
        send_sem=send,
        recv_sem=recv,
        device_id=(lax.rem(s + 1, PARTS), c),
        device_id_type=MESH,
    ).wait()


def chan_copy(buf, owner, piece, lane, send, recv, target):
    part = buf.at[owner, pl.ds(piece * PIECE, PIECE)]
    return pltpu.make_async_remote_copy(
        src_ref=part,
        dst_ref=part,
        send_sem=send.at[lane, piece],
        recv_sem=recv.at[lane, piece],
        device_id=target,
        device_id_type=MESH,
    )


def gather_copy(buf, piece, lane, send, recv):
    s, c = place()
    across, beside = lax.rem(c + 2, 4), c + 1 - 2 * lax.rem(c, 2)
    owner = across if lane == 2 else c
    target = across if lane == 0 else beside
    return chan_copy(buf, owner, piece, lane, send, recv, (s, target))


def gather_start(buf, piece, send, recv):
    gather_copy(buf, piece, 0, send, recv).start()
    gather_copy(buf, piece, 1, send, recv).start()


def gather_forward(buf, piece, send, recv):
    gather_copy(buf, piece, 0, send, recv).wait_recv()
    gather_copy(buf, piece, 2, send, recv).start()


def gather_finish(buf, piece, send, recv):
    gather_copy(buf, piece, 1, send, recv).wait()
    gather_copy(buf, piece, 2, send, recv).wait()
    gather_copy(buf, piece, 0, send, recv).wait_send()


def bits(mask):
    return half(mask.astype(jnp.float32))


def index_pair(shape):
    return lax.broadcasted_iota(jnp.int32, shape, 0), lax.broadcasted_iota(jnp.int32, shape, 1)


def same_place():
    row, col = index_pair((ROWS, ROWS))
    return jnp.bitwise_and(row, 7) == jnp.bitwise_and(col, 7)


def reorder(transposed):
    row, col = index_pair((ROWS, ROWS))
    if transposed:
        row, col = col, row
    return bits(col == jnp.bitwise_and(row, 7) * 64 + lax.shift_right_logical(row, 3))


def widen():
    row, col = index_pair((64, ROWS))
    return bits(row == lax.shift_right_logical(col, 3))


def spread_two(f2):
    wide = half(dot(f2.reshape(ROWS, 64), widen()))
    return half(jnp.where(same_place(), dot(reorder(False), wide), 0.0))


def gather_two(product):
    tall = half(dot_rows(half(jnp.where(same_place(), product, 0.0)), widen()))
    return half(dot(reorder(True), tall))


def remote(src, dst, send, recv, target):
    return pltpu.make_async_remote_copy(
        src_ref=src, dst_ref=dst, send_sem=send, recv_sem=recv,
        device_id=target, device_id_type=MESH,
    )


def axis_place(axis):
    s, _ = place()
    return lax.rem(s, 4) if axis == 0 else lax.div(s, 8)


def axis_peer(axis, step):
    s, c = place()
    here = axis_place(axis)
    there = lax.rem(here + step, 4)
    return s + (there - here) * (1 if axis == 0 else 8), c


class Ring:
    def __init__(self, view, early, late, send, recv, axis):
        self.view, self.early, self.late = view, early, late
        self.send, self.recv = send, recv
        self.here = axis_place(axis)
        self.ahead, self.behind = axis_peer(axis, 1), axis_peer(axis, 3)

    def copy(self, index):
        after, across, before = [lax.rem(self.here + k, 4) for k in (1, 2, 3)]
        src, dst, target = (
            lambda: (self.view(0, across), self.early.at[0], self.ahead),
            lambda: (self.view(1, across), self.early.at[1], self.behind),
            lambda: (self.view(1, after), self.late.at[0, 1], self.ahead),
            lambda: (self.view(0, before), self.late.at[1, 0], self.behind),
            lambda: (self.view(0, after), self.late.at[0, 0], self.ahead),
            lambda: (self.view(1, before), self.late.at[1, 1], self.behind),
        )[index]()
        return remote(src, dst, self.send.at[index], self.recv.at[index], target)

    def start(self):
        for index in range(4):
            self.copy(index).start()

    def middle(self):
        after, before = lax.rem(self.here + 1, 4), lax.rem(self.here + 3, 4)
        for way, owner in ((0, after), (1, before)):
            self.copy(way).wait_recv()
            mine = self.view(way, owner)
            mine[...] = half(full(mine[...]) + full(self.early[way]))
            self.copy(4 + way).start()

    def arrive(self):
        for index in range(2, 6):
            self.copy(index).wait_recv()

    def total(self, part):
        return full(self.view(part, self.here)[...]) + (
            full(self.late[0, part]) + full(self.late[1, part])
        )

    def settle(self):
        for index in range(6):
            self.copy(index).wait_send()


class Grads:
    def __init__(self, own, bufs, sems, result):
        self.own, self.result = own, result
        self.early_one, self.late_one, self.early_two, self.late_two, self.last = bufs
        self.send, self.recv = sems

    def ring(self, unit, stage):
        slot, first = unit % SLOTS, unit % 2
        sems = [s.at[unit, stage] for s in (self.send, self.recv)]
        if stage == 0:
            view = lambda part, owner: self.own.at[slot, part, owner]
            return Ring(view, self.early_one.at[unit], self.late_one.at[unit], *sems, first)
        here = axis_place(first)
        view = lambda part, owner: self.own.at[slot, part, here, owner]
        return Ring(view, self.early_two.at[unit], self.late_two.at[unit], *sems, 1 - first)

    def multiply(self, unit, left, right):
        slot = unit % SLOTS
        own = self.own
        if unit >= SLOTS:
            self.last_copy(unit - SLOTS).wait_send()

        @pl.loop(0, 4)
        def _(z):
            rows = pl.ds(pl.multiple_of(z * 512, 512), 512)
            tile = half(dot(left[rows, :], right).reshape(2, 4, SHARE, BLOCK))
            if unit % 2 == 0:
                own[slot, :, :, z] = tile
            else:
                own[slot, :, z] = tile

        self.ring(unit, 0).start()

    def middle(self, unit, stage):
        self.ring(unit, stage).middle()

    def turn(self, unit):
        ring = self.ring(unit, 0)
        ring.arrive()

        @pl.loop(0, 2)
        def _(part):
            ring.view(part, ring.here)[...] = half(ring.total(part))

        self.ring(unit, 1).start()
        ring.settle()

    def last_copy(self, unit):
        s, c = place()
        near = lax.rem(lax.div(s, 4), 2)
        ring = self.ring(unit, 1)
        sems = [s.at[unit, 2, 0] for s in (self.send, self.recv)]
        src = ring.view(1 - near, ring.here)
        return remote(src, self.last.at[unit], *sems, (s + 4 - 8 * near, c))

    def finish(self, unit):
        s, _ = place()
        near = lax.rem(lax.div(s, 4), 2)
        ring = self.ring(unit, 1)
        ring.arrive()
        ring.view(1 - near, ring.here)[...] = half(ring.total(1 - near))
        self.last_copy(unit).start()
        self.result[unit // 2, :, pl.ds(unit % 2 * BLOCK, BLOCK)] = ring.total(near)
        ring.settle()

    def close(self, unit):
        self.last_copy(unit).wait_recv()
        if unit + SLOTS >= UNITS:
            self.last_copy(unit).wait_send()
        cols = pl.ds(unit % 2 * BLOCK, BLOCK)
        self.result[unit // 2, :, cols] = self.result[unit // 2, :, cols] + full(self.last[unit])


class ChanSum:
    def __init__(self, part, near, far, send, recv):
        self.part, self.near, self.far, self.send, self.recv = part, near, far, send, recv
        s, c = place()
        self.high, self.core = lax.div(c, 2), lax.rem(c, 2)
        self.beside, self.across = (s, c + 1 - 2 * self.core), (s, lax.rem(c + 2, 4))

    def near_copy(self, high):
        return remote(
            self.part.at[high * 2 + 1 - self.core], self.near.at[high],
            self.send.at[high], self.recv.at[high], self.beside,
        )

    def far_copy(self):
        return remote(
            self.part.at[(1 - self.high) * 2 + self.core], self.far,
            self.send.at[2], self.recv.at[2], self.across,
        )

    def start(self):
        for high in range(2):
            self.near_copy(high).start()

    def onward(self):
        for high in range(2):
            self.near_copy(high).wait()
        other = 1 - self.high
        slot = other * 2 + self.core
        self.part[slot] = half(full(self.part[slot]) + full(self.near[other]))
        self.far_copy().start()

    def arrive(self):
        self.far_copy().wait()

    def total(self, rows):
        mine = full(self.part[self.high * 2 + self.core, rows])
        return mine + full(self.near[self.high, rows]) + full(self.far[rows])


class PairSum:
    def __init__(self, part, got, send, recv):
        self.part, self.got, self.send, self.recv = part, got, send, recv
        s, c = place()
        self.targets = (s, c + 1 - 2 * lax.rem(c, 2)), (s, lax.rem(c + 2, 4))

    def copy(self, step):
        return remote(
            self.part.at[step], self.got.at[step],
            self.send.at[step], self.recv.at[step], self.targets[step],
        )

    def start(self, values):
        self.part[0] = values
        self.copy(0).start()

    def onward(self):
        self.copy(0).wait()
        self.part[1] = half(full(self.part[0]) + full(self.got[0]))
        self.copy(1).start()

    def finish(self):
        self.copy(1).wait()
        return full(self.part[1]) + full(self.got[1])


class SeqSum:
    def __init__(self, slots, send, recv):
        self.slots, self.send, self.recv = slots, send, recv

    def copy(self, axis, step):
        mine = self.slots.at[axis, axis_place(axis)]
        return remote(
            mine, mine, self.send.at[axis, step], self.recv.at[axis, step],
            axis_peer(axis, step),
        )

    def pair_copy(self):
        s, c = place()
        near = lax.rem(lax.div(s, 4), 2)
        mine = self.slots.at[2, near]
        return remote(
            mine, mine, self.send.at[2, 1], self.recv.at[2, 1], (s + 4 - 8 * near, c)
        )

    def start(self, values):
        self.slots[0, axis_place(0)] = values
        for step in range(1, 4):
            self.copy(0, step).start()

    def take(self, axis):
        for step in range(1, 4):
            self.copy(axis, step).wait()
        return (self.slots[axis, 0] + self.slots[axis, 1]) + (
            self.slots[axis, 2] + self.slots[axis, 3]
        )

    def second(self):
        self.slots[1, axis_place(1)] = self.take(0)
        for step in range(1, 4):
            self.copy(1, step).start()

    def third(self):
        s, _ = place()
        self.slots[2, lax.rem(lax.div(s, 4), 2)] = self.take(1)
        self.pair_copy().start()

    def finish(self):
        self.pair_copy().wait()
        return self.slots[2, 0] + self.slots[2, 1]


def layer(
    x, og, f1, f2, scale, shift, gain, wg_hbm, wu_hbm, wd_hbm,
    layer_out, input_grad, one_grad, two_grad, vectors, grads_out,
    wg, wu, wd, cot, flipped, wm, normed, gate_pre, up_pre, hidden, gate_back, up_back,
    inv, dots, first_cols, seqmix, back_cols, first_back, src, big_two,
    sum_near, sum_far, own, early_one, late_one, early_two, late_two, last,
    one_part, one_got, two_part, two_got, slots,
    w_sem, swap_send, swap_recv, gs, gr, hs, hr, grad_send, grad_recv, sum_send, sum_recv,
    dot_send, dot_recv, pair_send, pair_recv, vec_send, vec_recv,
):
    s, c = place()
    top, low = pl.ds(0, 256), pl.ds(256, 256)
    swap = lambda k: (swap_send.at[k], swap_recv.at[k])
    weights = [
        pltpu.make_async_copy(a, b, w_sem.at[k])
        for k, (a, b) in enumerate(((wg_hbm, wg), (wu_hbm, wu), (wd_hbm, wd)))
    ]
    for copy in weights:
        copy.start()
    for piece in range(PIECES):
        cot[c, pl.ds(piece * PIECE, PIECE)] = half(inside(og, piece))
    src[0] = half(interleaved(dot(f1[0], x[top]), dot(f1[1], x[low])))
    greet()
    swap_start(src.at[0], first_cols, *swap(0))
    for piece in range(PIECES):
        gather_start(cot, piece, hs, hr)
    big_two[0] = spread_two(f2[...])
    big_two[1] = big_two[0].T
    swap_wait(src.at[0], first_cols, *swap(0))
    src[1] = half(dot(big_two[0], first_cols[...]))
    swap_start(src.at[1], seqmix, *swap(1))
    for piece in range(PIECES):
        gather_forward(cot, piece, hs, hr)
    swap_wait(src.at[1], seqmix, *swap(1))
    for piece in range(PIECES):
        rows = pl.ds(piece * PIECE, PIECE)
        xf = inside(x, piece)
        opening = jax.nn.sigmoid(xf * scale[...] + shift[...])
        wm[c, rows] = half(xf + opening * full(seqmix[rows]))
        gather_start(wm, piece, gs, gr)
    for piece in range(PIECES):
        gather_finish(cot, piece, hs, hr)
    for k in range(4):
        flipped[pl.ds(k * BLOCK, BLOCK), :] = cot[k].T
    for piece in range(PIECES):
        gather_forward(wm, piece, gs, gr)
    for copy in weights:
        copy.wait()

    for part in range(2):
        for piece in (2 * part, 2 * part + 1):
            gather_finish(wm, piece, gs, gr)

        @pl.loop(0, 4)
        def _(k):
            rows = pl.ds(pl.multiple_of(part * 256 + k * 64, 64), 64)
            blocks = [full(wm[chan, rows]) for chan in range(4)]
            squares = sum(jnp.sum(b * b, axis=1, keepdims=True) for b in blocks)
            scaled = lax.rsqrt(squares / (4 * BLOCK) + 1e-05)
            inv[rows] = jnp.broadcast_to(scaled, (64, 128))
            for chan in range(4):
                normed[chan, rows] = half(blocks[chan] * scaled * gain[chan])

        rows = pl.ds(part * 256, 256)
        for k in range(2):
            cols = pl.ds(k * BLOCK, BLOCK)
            gate = up = 0.0
            for chan in range(4):
                deep = pl.ds(chan * BLOCK, BLOCK)
                gate = gate + dot(normed[chan, rows], wg[deep, cols])
                up = up + dot(normed[chan, rows], wu[deep, cols])
            gate_pre[rows, cols] = gate
            up_pre[rows, cols] = up
            hidden[rows, cols] = half(gate * jax.nn.sigmoid(gate) * up)

    grads = Grads(
        own, (early_one, late_one, early_two, late_two, last), (grad_send, grad_recv), grads_out
    )
    lows, highs = pl.ds(0, BLOCK), pl.ds(BLOCK, BLOCK)
    grads.multiply(0, flipped, hidden[:, lows])
    grads.multiply(1, flipped, hidden[:, highs])
    for k in range(4):
        flipped[pl.ds(k * BLOCK, BLOCK), :] = normed[k].T

    for part in range(2):
        rows = pl.ds(part * 256, 256)
        products = 0.0
        for k in range(2):
            cols = pl.ds(k * BLOCK, BLOCK)
            hidden_grad = 0.0
            for chan in range(4):
                deep = pl.ds(chan * BLOCK, BLOCK)
                hidden_grad = hidden_grad + dot_rows(cot[chan, rows], wd[cols, deep])
            gate, up = gate_pre[rows, cols], up_pre[rows, cols]
            s_gate = jax.nn.sigmoid(gate)
            back = half(hidden_grad * up * s_gate * (1.0 + gate * (1.0 - s_gate)))
            gate_back[rows, cols] = back
            products = products + jnp.sum(full(back) * gate, axis=1, keepdims=True)
            back = half(hidden_grad * gate * s_gate)
            up_back[rows, cols] = back
            products = products + jnp.sum(full(back) * up, axis=1, keepdims=True)
        turned = jnp.broadcast_to(products, (256, 128)).T
        dots[c, :, rows] = turned[:8]
    dot_copies = [
        remote(dots.at[c], dots.at[c], dot_send.at[k], dot_recv.at[k], (s, lax.rem(c + k, 4)))
        for k in range(1, 4)
    ]
    for copy in dot_copies:
        copy.start()

    def joint_back(chan):
        rows = pl.ds(pl.multiple_of(chan * BLOCK, BLOCK), BLOCK)
        return half(dot_rows(gate_back[...], wg[rows, :]) + dot_rows(up_back[...], wu[rows, :]))

    @pl.loop(0, 4)
    def _(chan):
        normed[chan] = joint_back(chan)

    back_sum = ChanSum(
        normed, sum_near.at[0], sum_far.at[0], sum_send.at[0], sum_recv.at[0]
    )
    back_sum.start()
    grads.middle(0, 0)
    grads.middle(1, 0)
    grads.multiply(2, flipped, gate_back[:, lows])
    grads.multiply(3, flipped, gate_back[:, highs])
    back_sum.onward()

    for chan in range(4):
        cols = pl.ds(chan * BLOCK, BLOCK)
        cot[chan] = half(dot(hidden[...], wd[:, cols]))
    out_sum = ChanSum(cot, sum_near.at[1], sum_far.at[1], sum_send.at[1], sum_recv.at[1])
    out_sum.start()
    grads.turn(0)
    grads.turn(1)
    out_sum.onward()
    grads.middle(2, 0)
    grads.middle(3, 0)
    for copy in dot_copies:
        copy.wait()
    row_total = (dots[0] + dots[1]) + (dots[2] + dots[3])
    up_pre[:, pl.ds(0, 128)] = jnp.broadcast_to(row_total[:1], (128, ROWS)).T
    grads.middle(0, 1)
    grads.middle(1, 1)

    back_sum.arrive()
    sums = [0.0, 0.0, 0.0]
    for piece in range(PIECES):
        rows = pl.ds(piece * PIECE, PIECE)
        normed_grad = back_sum.total(rows)
        scaled, total = inv[rows][:, :1], up_pre[rows, pl.ds(0, 128)][:, :1]
        mixed, xf = full(wm[c, rows]), inside(x, piece)
        mixed_grad = inside(og, piece) + scaled * gain[c] * normed_grad
        mixed_grad = mixed_grad - mixed * (scaled * scaled * total / (4 * BLOCK))
        opening = jax.nn.sigmoid(xf * scale[...] + shift[...])
        src[0, rows] = half(mixed_grad * opening)
        pre_grad = mixed_grad * full(seqmix[rows]) * opening * (1.0 - opening)
        gate_pre[rows, lows] = mixed_grad + pre_grad * scale[...]
        for k, term in enumerate((pre_grad * xf, pre_grad, normed_grad * mixed * scaled)):
            sums[k] = sums[k] + jnp.sum(term, axis=0, keepdims=True)
    swap_start(src.at[0], back_cols, *swap(2))
    vector_sum = SeqSum(slots, vec_send, vec_recv)
    row, _ = index_pair((8, BLOCK))
    vector_sum.start(
        jnp.where(row == 0, sums[0], jnp.where(row == 1, sums[1], jnp.where(row == 2, sums[2], 0.0)))
    )
    grads.finish(0)
    grads.finish(1)
    grads.multiply(4, flipped, up_back[:, lows])
    grads.multiply(5, flipped, up_back[:, highs])
    swap_wait(src.at[0], back_cols, *swap(2))
    src[1] = half(dot(big_two[1], back_cols[...]))
    swap_start(src.at[1], first_back, *swap(3))
    vector_sum.second()
    two_sum = PairSum(two_part, two_got, pair_send.at[0], pair_recv.at[0])
    two_sum.start(gather_two(dot_rows(back_cols[...], first_cols[...])))
    grads.turn(2)
    grads.turn(3)
    grads.middle(4, 0)
    grads.middle(5, 0)
    two_sum.onward()
    vector_sum.third()
    out_sum.arrive()
    plain_out = deal(full(wm[c]) + out_sum.total(pl.ds(0, ROWS)))
    layer_out[top] = half(plain_out[0])
    layer_out[low] = half(plain_out[1])
    grads.middle(2, 1)
    grads.middle(3, 1)
    swap_wait(src.at[1], first_back, *swap(3))
    one_sum = PairSum(one_part, one_got, pair_send.at[1], pair_recv.at[1])
    blocks = [half(b) for b in deal(full(first_back[...]))]
    one_sum.start(
        jnp.concatenate(
            [half(dot_rows(blocks[0], x[top])), half(dot_rows(blocks[1], x[low]))], axis=0
        )
    )
    kept_plain = deal(gate_pre[:, lows])
    for k, rows in enumerate((top, low)):
        input_grad[rows] = half(kept_plain[k] + dot(f1[k].T, blocks[k]))
    grads.finish(2)
    grads.finish(3)
    one_sum.onward()
    two_grad[...] = two_sum.finish()
    vectors[...] = vector_sum.finish()
    grads.turn(4)
    grads.turn(5)
    grads.middle(4, 1)
    grads.middle(5, 1)
    one_grad[...] = one_sum.finish()
    for unit in range(4):
        grads.close(unit)
    grads.finish(4)
    grads.finish(5)
    grads.close(4)
    grads.close(5)


def on_device(
    layer_in, factor_one, factor_two, gate_scale, gate_shift, norm_gain, w_gate, w_up, w_down, out_grad
):
    vmem, away = pl.BlockSpec(memory_space=pltpu.VMEM), pl.BlockSpec(memory_space=pl.ANY)
    bf, f32 = jnp.bfloat16, jnp.float32
    dma = pltpu.SemaphoreType.DMA
    square = pltpu.VMEM((ROWS, BLOCK), bf)
    whole = pltpu.VMEM((4, ROWS, BLOCK), bf)
    flipped = pltpu.VMEM((4 * BLOCK, ROWS), bf)
    wide = pltpu.VMEM((ROWS, HIDDEN), bf)
    wide_float = pltpu.VMEM((ROWS, HIDDEN), f32)
    out = jax.ShapeDtypeStruct
    outs = pl.pallas_call(
        layer,
        out_shape=(
            out((ROWS, BLOCK), bf),
            out((ROWS, BLOCK), bf),
            out((2 * 256, 256), f32),
            out((ROWS, 64), f32),
            out((8, BLOCK), f32),
            out((3, SHARE, HIDDEN), f32),
        ),
        in_specs=[vmem] * 7 + [away] * 3,
        out_specs=(vmem,) * 6,
        scratch_shapes=[
            pltpu.VMEM((4 * BLOCK, HIDDEN), bf),
            pltpu.VMEM((4 * BLOCK, HIDDEN), bf),
            pltpu.VMEM((HIDDEN, 4 * BLOCK), bf),
            whole, flipped, whole, whole,
            wide_float, wide_float, wide, wide, wide,
            pltpu.VMEM((ROWS, 128), f32),
            pltpu.VMEM((4, 8, ROWS), f32),
            square, square, square, square,
            pltpu.VMEM((2, ROWS, BLOCK), bf),
            pltpu.VMEM((2, ROWS, BLOCK), bf),
            pltpu.VMEM((2, 2, ROWS, BLOCK), bf),
            pltpu.VMEM((2, ROWS, BLOCK), bf),
            pltpu.VMEM((SLOTS, 2, 4, 4, SHARE, BLOCK), bf),
            pltpu.VMEM((UNITS, 2, 4, SHARE, BLOCK), bf),
            pltpu.VMEM((UNITS, 2, 2, 4, SHARE, BLOCK), bf),
            pltpu.VMEM((UNITS, 2, SHARE, BLOCK), bf),
            pltpu.VMEM((UNITS, 2, 2, SHARE, BLOCK), bf),
            pltpu.VMEM((UNITS, SHARE, BLOCK), bf),
            pltpu.VMEM((2, 2 * 256, 256), bf),
            pltpu.VMEM((2, 2 * 256, 256), bf),
            pltpu.VMEM((2, ROWS, 64), bf),
            pltpu.VMEM((2, ROWS, 64), bf),
            pltpu.VMEM((3, 4, 8, BLOCK), f32),
            dma((3,)),
            dma((4,)), dma((4,)),
            dma((3, PIECES)), dma((3, PIECES)), dma((3, PIECES)), dma((3, PIECES)),
            dma((UNITS, 3, 6)), dma((UNITS, 3, 6)),
            dma((2, 3)), dma((2, 3)),
            dma((4,)), dma((4,)),
            dma((2, 2)), dma((2, 2)),
            dma((3, 4)), dma((3, 4)),
        ],
        compiler_params=pltpu.CompilerParams(
            collective_id=0, has_side_effects=True, vmem_limit_bytes=VMEM_LIMIT
        ),
        name="layer",
    )(
        layer_in, out_grad, factor_one, factor_two,
        gate_scale.reshape(1, -1), gate_shift.reshape(1, -1), norm_gain.reshape(4, 1, -1),
        w_gate, w_up, w_down,
    )
    layer_out, input_grad, one_grad, two_grad, vectors, grads = outs
    return (
        layer_out,
        input_grad,
        one_grad.reshape(factor_one.shape),
        two_grad.reshape(factor_two.shape),
        vectors[0],
        vectors[1],
        vectors[2],
        grads[1],
        grads[2],
        grads[0].T,
    )


def solution(mesh):
    return jax.shard_map(
        on_device,
        mesh=mesh,
        in_specs=(
            P("seq", "chan"),
            P("seq", None, None),
            P("seq", None, None),
            P("chan"),
            P("chan"),
            P(),
            P(None, "chan"),
            P(None, "chan"),
            P("chan", None),
            P("seq", "chan"),
        ),
        out_specs=(
            P("seq", "chan"),
            P("seq", "chan"),
            P("seq", None, None),
            P("seq", None, None),
            P("chan"),
            P("chan"),
            P("chan"),
            P("seq", "chan"),
            P("seq", "chan"),
            P("chan", "seq"),
        ),
        check_vma=False,
    )
```

time: 449 us -> 163 us (0.36)
  waiting for transfers between devices: 173 us -> 0 us
  Pallas kernels: 47.1 us -> 149 us
  blocking collectives: 92 us -> 0 us
  matrix products: 43.4 us -> 0 us
  local copies, waits for them, and re-layouts: 39.4 us -> 9.73 us
  other arithmetic: 22.9 us -> 0 us
  between operations: 15.6 us -> 0.67 us
  starting transfers between devices: 13.9 us -> 0 us
    pallas_call x1, Pallas kernels: 47.1 us -> 149 us  [on_device(): pl.pallas_call(layer, out_shape=(out((ROWS, BLOCK), bf), out((ROWS, BLOCK...]
    unnamed x5 -> x0, waiting for transfers between devices: 102 us -> none
    psum x2 -> x0, blocking collectives: 92 us -> none  [the longest x1 81.9 us: on_device(): lax.psum((scale_local, shift_local, gain_local), 'seq')]
    reduce_scatter x2 -> x0, waiting for transfers between devices: 62.9 us -> none  [the longest x1 34 us: on_device(): lax.psum_scatter(total + lax.dot_general(w_up, up_back, contract, preferr...]
    dot_general x13 -> x0, matrix products: 43.4 us -> none  [the longest x1 6.53 us: on_device(): lax.dot_general(normed, up_back, dims_first, preferred_element_type=jnp.f...]
    unnamed x65 -> x6, local copies, waits for them, and re-layouts: 31.8 us -> 6.31 us
    all_to_all x2 -> x0, starting transfers between devices: 13.3 us -> none  [the longest x1 9.12 us: on_device(): lax.all_to_all(seqmix_grad.reshape(block_count, block, width), 'seq', spl...]
    concatenate x1 -> x0, other arithmetic: 11.4 us -> none  [on_device(): jnp.concatenate([jnp.concatenate([gate_term, up_term], axis=1), lax.dot_g...]
  transfers between devices with their start and end apart: 6 -> 0, of which waited for: 5 -> 0; matrix products, arithmetic and copies ran while one was open for 14% -> 0% of each run, Pallas kernels for 0% -> 0%
where the time goes in v2:
time: 163 us; the launch traced here: 160 us
  Pallas kernels  149 us (91%)
  local copies, waits for them, and re-layouts  9.73 us (6%)
    pallas_call x1, Pallas kernels, on_device(): pl.pallas_call(layer, out_shape=(out((ROWS, BLOCK), bf), out((ROWS, BLOCK...  149 us
    unnamed x6, local copies, waits for them, and re-layouts  6.31 us

profile of v2, /device:TPU:16, one launch (start us, length us, event | category | flops | bytes accessed | tf_op | source)
XLA Modules:
  0.0 159.8 jit_solution(7622633722590618699)
XLA Ops:
  0.6 149.4 %layer.1 = (bf16[512,512]{1,0:T(8,128)(2,1)}, bf16[512,512]{1,0:T(8,128)(2,1)}, f32[512,256]{1,0:T(8,128)}, f32[512,64]{1,0:T(8,128)}, f32[8,512]{1,0:T(8,128)}, /*index=5*/f32[3,64,1024]{2,1,0:T(8,128)}) custom-call(bf16[512,512]{1,0:T(8,128)(2,1)} %x.1, bf16[512,512]{1,0:T(8,128)(2,1)} %og.1, bf16[2,256,256]{2,1,0:T(8,128)(2,1)} %f1.1, ...), custom_call_target="tpu_custom_call" | custom-call | tf_op jit(solution)/shard_map/layer/pallas_call | solution.py:659
  150.0 0.0 copy-start
  150.0 1.4 fusion
  151.5 2.0 %slice_bitcast_fusion = (f32[1024,64]{0,1:T(8,128)}, f32[64,1024]{1,0:T(8,128)}, f32[64,1024]{1,0:T(8,128)}) fusion(f32[3,64,1024]{2,1,0:T(8,128)} %get-tuple-element.21), kind=kLoop, calls=%fused_computation | loop fusion | bytes 1572864 | tf_op jit(solution)/shard_map/transpose | solution.py:724
  153.5 1.9 %copy.24 = bf16[512,512]{1,0:T(8,128)(2,1)} copy(bf16[512,512]{1,0:T(8,128)(2,1)} %get-tuple-element.38) | data formatting | bytes 1048576
  155.3 1.9 %copy.25 = bf16[512,512]{1,0:T(8,128)(2,1)} copy(bf16[512,512]{1,0:T(8,128)(2,1)} %get-tuple-element.39) | data formatting | bytes 1048576
  157.2 1.9 %copy.26 = f32[2,256,256]{2,1,0:T(8,128)} copy(f32[2,256,256]{2,1,0:T(8,128)} %bitcast.16) | data formatting | bytes 1048576
  159.1 0.0 copy-done
  159.1 0.7 copy.27
Async XLA Ops:
  150.0 9.0 %copy-start = (f32[512,64]{1,0:T(8,128)S(1)}, f32[512,64]{1,0:T(8,128)}, u32[]{:S(2)}) copy-start(f32[512,64]{1,0:T(8,128)} %get-tuple-element.19) | copy-start | bytes 393220

commit v3 on v2

--- a/solution.py
+++ b/solution.py
@@ -16,6 +16,8 @@
 UNITS = 6
 SLOTS = 4
 SHARE = 64
+EARLY = 2
+OUTPUTS = 10
 VMEM_LIMIT = 67000000
 
 
@@ -69,7 +71,10 @@
     for step in range(1, 4):
         target = (s, lax.rem(c + step, 4))
         pl.semaphore_signal(barrier, inc=1, device_id=target, device_id_type=MESH)
-    pl.semaphore_wait(barrier, PARTS - 1 + 3)
+
+
+def greeted():
+    pl.semaphore_wait(pltpu.get_barrier_semaphore(), PARTS - 1 + 3)
 
 
 def slab(index):
@@ -244,8 +249,9 @@
 
 
 class Grads:
-    def __init__(self, own, bufs, sems, result):
-        self.own, self.result = own, result
+    def __init__(self, own, mid, bufs, sems, result, out, out_sem):
+        self.own, self.mid, self.result = own, mid, result
+        self.out, self.out_sem = out, out_sem
         self.early_one, self.late_one, self.early_two, self.late_two, self.last = bufs
         self.send, self.recv = sems
 
@@ -255,20 +261,14 @@
         if stage == 0:
             view = lambda part, owner: self.own.at[slot, part, owner]
             return Ring(view, self.early_one.at[unit], self.late_one.at[unit], *sems, first)
-        here = axis_place(first)
-        view = lambda part, owner: self.own.at[slot, part, here, owner]
+        view = lambda part, owner: self.mid.at[slot, part, owner]
         return Ring(view, self.early_two.at[unit], self.late_two.at[unit], *sems, 1 - first)
 
     def multiply(self, unit, left, right):
         slot = unit % SLOTS
         own = self.own
-        if unit >= SLOTS:
-            self.last_copy(unit - SLOTS).wait_send()
-
-        @pl.loop(0, 4)
-        def _(z):
-            rows = pl.ds(pl.multiple_of(z * 512, 512), 512)
-            tile = half(dot(left[rows, :], right).reshape(2, 4, SHARE, BLOCK))
+        for z in range(4):
+            tile = half(dot(left[pl.ds(z * 512, 512), :], right).reshape(2, 4, SHARE, BLOCK))
             if unit % 2 == 0:
                 own[slot, :, :, z] = tile
             else:
@@ -282,10 +282,12 @@
     def turn(self, unit):
         ring = self.ring(unit, 0)
         ring.arrive()
+        if unit >= SLOTS:
+            self.last_copy(unit - SLOTS).wait_send()
 
         @pl.loop(0, 2)
         def _(part):
-            ring.view(part, ring.here)[...] = half(ring.total(part))
+            self.mid[unit % SLOTS, part] = half(ring.total(part))
 
         self.ring(unit, 1).start()
         ring.settle()
@@ -305,15 +307,24 @@
         ring.arrive()
         ring.view(1 - near, ring.here)[...] = half(ring.total(1 - near))
         self.last_copy(unit).start()
-        self.result[unit // 2, :, pl.ds(unit % 2 * BLOCK, BLOCK)] = ring.total(near)
+        self.result[self.place(unit)] = ring.total(near)
         ring.settle()
+
+    def place(self, unit):
+        return pl.ds(unit * SHARE, SHARE), pl.ds(BLOCK, BLOCK)
+
+    def out_copy(self, unit):
+        cols = pl.ds(unit % 2 * BLOCK, BLOCK)
+        dst = self.out[unit // 2].at[:, cols]
+        return pltpu.make_async_copy(self.result.at[self.place(unit)], dst, self.out_sem.at[unit])
 
     def close(self, unit):
         self.last_copy(unit).wait_recv()
         if unit + SLOTS >= UNITS:
             self.last_copy(unit).wait_send()
-        cols = pl.ds(unit % 2 * BLOCK, BLOCK)
-        self.result[unit // 2, :, cols] = self.result[unit // 2, :, cols] + full(self.last[unit])
+        place = self.place(unit)
+        self.result[place] = self.result[place] + full(self.last[unit])
+        self.out_copy(unit).start()
 
 
 class ChanSum:
@@ -429,16 +440,18 @@
 
 def layer(
     x, og, f1, f2, scale, shift, gain, wg_hbm, wu_hbm, wd_hbm,
-    layer_out, input_grad, one_grad, two_grad, vectors, grads_out,
+    layer_out, input_grad, one_grad, two_grad, scale_grad, shift_grad, gain_grad, down_out, gate_out, up_out,
     wg, wu, wd, cot, flipped, wm, normed, gate_pre, up_pre, hidden, gate_back, up_back,
     inv, dots, first_cols, seqmix, back_cols, first_back, src, big_two,
-    sum_near, sum_far, own, early_one, late_one, early_two, late_two, last,
+    sum_near, sum_far, own, mid, early_one, late_one, early_two, late_two, last,
     one_part, one_got, two_part, two_got, slots,
     w_sem, swap_send, swap_recv, gs, gr, hs, hr, grad_send, grad_recv, sum_send, sum_recv,
-    dot_send, dot_recv, pair_send, pair_recv, vec_send, vec_recv,
+    dot_send, dot_recv, pair_send, pair_recv, vec_send, vec_recv, out_sem,
 ):
     s, c = place()
+    greet()
     top, low = pl.ds(0, 256), pl.ds(256, 256)
+    lows, highs = pl.ds(0, BLOCK), pl.ds(BLOCK, BLOCK)
     swap = lambda k: (swap_send.at[k], swap_recv.at[k])
     weights = [
         pltpu.make_async_copy(a, b, w_sem.at[k])
@@ -446,19 +459,19 @@
     ]
     for copy in weights:
         copy.start()
+    src[0] = half(interleaved(dot(f1[0], x[top]), dot(f1[1], x[low])))
+    greeted()
+    swap_start(src.at[0], first_cols, *swap(0))
     for piece in range(PIECES):
         cot[c, pl.ds(piece * PIECE, PIECE)] = half(inside(og, piece))
-    src[0] = half(interleaved(dot(f1[0], x[top]), dot(f1[1], x[low])))
-    greet()
-    swap_start(src.at[0], first_cols, *swap(0))
-    for piece in range(PIECES):
+    for piece in range(EARLY):
         gather_start(cot, piece, hs, hr)
     big_two[0] = spread_two(f2[...])
     big_two[1] = big_two[0].T
     swap_wait(src.at[0], first_cols, *swap(0))
     src[1] = half(dot(big_two[0], first_cols[...]))
     swap_start(src.at[1], seqmix, *swap(1))
-    for piece in range(PIECES):
+    for piece in range(EARLY):
         gather_forward(cot, piece, hs, hr)
     swap_wait(src.at[1], seqmix, *swap(1))
     for piece in range(PIECES):
@@ -467,16 +480,14 @@
         opening = jax.nn.sigmoid(xf * scale[...] + shift[...])
         wm[c, rows] = half(xf + opening * full(seqmix[rows]))
         gather_start(wm, piece, gs, gr)
-    for piece in range(PIECES):
-        gather_finish(cot, piece, hs, hr)
-    for k in range(4):
-        flipped[pl.ds(k * BLOCK, BLOCK), :] = cot[k].T
+    for piece in range(EARLY, PIECES):
+        gather_start(cot, piece, hs, hr)
     for piece in range(PIECES):
         gather_forward(wm, piece, gs, gr)
     for copy in weights:
         copy.wait()
 
-    for part in range(2):
+    def norm_rows(part):
         for piece in (2 * part, 2 * part + 1):
             gather_finish(wm, piece, gs, gr)
 
@@ -490,23 +501,34 @@
             for chan in range(4):
                 normed[chan, rows] = half(blocks[chan] * scaled * gain[chan])
 
-        rows = pl.ds(part * 256, 256)
-        for k in range(2):
-            cols = pl.ds(k * BLOCK, BLOCK)
-            gate = up = 0.0
-            for chan in range(4):
-                deep = pl.ds(chan * BLOCK, BLOCK)
-                gate = gate + dot(normed[chan, rows], wg[deep, cols])
-                up = up + dot(normed[chan, rows], wu[deep, cols])
-            gate_pre[rows, cols] = gate
-            up_pre[rows, cols] = up
-            hidden[rows, cols] = half(gate * jax.nn.sigmoid(gate) * up)
-
+    def expand(part, k):
+        rows, cols = pl.ds(part * 256, 256), pl.ds(k * BLOCK, BLOCK)
+        gate = up = 0.0
+        for chan in range(4):
+            deep = pl.ds(chan * BLOCK, BLOCK)
+            gate = gate + dot(normed[chan, rows], wg[deep, cols])
+            up = up + dot(normed[chan, rows], wu[deep, cols])
+        gate_pre[rows, cols] = gate
+        up_pre[rows, cols] = up
+        hidden[rows, cols] = half(gate * jax.nn.sigmoid(gate) * up)
+
+    norm_rows(0)
+    expand(0, 0)
+    expand(0, 1)
+    norm_rows(1)
+    expand(1, 0)
+    for piece in range(EARLY, PIECES):
+        gather_forward(cot, piece, hs, hr)
+    for piece in range(PIECES):
+        gather_finish(cot, piece, hs, hr)
+    for k in range(4):
+        flipped[pl.ds(k * BLOCK, BLOCK), :] = cot[k].T
     grads = Grads(
-        own, (early_one, late_one, early_two, late_two, last), (grad_send, grad_recv), grads_out
-    )
-    lows, highs = pl.ds(0, BLOCK), pl.ds(BLOCK, BLOCK)
+        own, mid, (early_one, late_one, early_two, late_two, last), (grad_send, grad_recv),
+        gate_pre, (down_out, gate_out, up_out), out_sem,
+    )
     grads.multiply(0, flipped, hidden[:, lows])
+    expand(1, 1)
     grads.multiply(1, flipped, hidden[:, highs])
     for k in range(4):
         flipped[pl.ds(k * BLOCK, BLOCK), :] = normed[k].T
@@ -536,41 +558,37 @@
     ]
     for copy in dot_copies:
         copy.start()
-
-    def joint_back(chan):
-        rows = pl.ds(pl.multiple_of(chan * BLOCK, BLOCK), BLOCK)
-        return half(dot_rows(gate_back[...], wg[rows, :]) + dot_rows(up_back[...], wu[rows, :]))
-
-    @pl.loop(0, 4)
-    def _(chan):
-        normed[chan] = joint_back(chan)
-
-    back_sum = ChanSum(
-        normed, sum_near.at[0], sum_far.at[0], sum_send.at[0], sum_recv.at[0]
-    )
-    back_sum.start()
     grads.middle(0, 0)
     grads.middle(1, 0)
     grads.multiply(2, flipped, gate_back[:, lows])
     grads.multiply(3, flipped, gate_back[:, highs])
-    back_sum.onward()
-
+
+    @pl.loop(0, 4)
+    def _(chan):
+        rows = pl.ds(pl.multiple_of(chan * BLOCK, BLOCK), BLOCK)
+        back = dot_rows(gate_back[...], wg[rows, :]) + dot_rows(up_back[...], wu[rows, :])
+        normed[chan] = half(back)
+
+    back_sum = ChanSum(
+        normed, sum_near.at[0], sum_far.at[0], sum_send.at[0], sum_recv.at[0]
+    )
+    back_sum.start()
     for chan in range(4):
         cols = pl.ds(chan * BLOCK, BLOCK)
         cot[chan] = half(dot(hidden[...], wd[:, cols]))
+    back_sum.onward()
     out_sum = ChanSum(cot, sum_near.at[1], sum_far.at[1], sum_send.at[1], sum_recv.at[1])
     out_sum.start()
     grads.turn(0)
     grads.turn(1)
-    out_sum.onward()
+    grads.multiply(4, flipped, up_back[:, lows])
+    grads.multiply(5, flipped, up_back[:, highs])
     grads.middle(2, 0)
     grads.middle(3, 0)
     for copy in dot_copies:
         copy.wait()
     row_total = (dots[0] + dots[1]) + (dots[2] + dots[3])
     up_pre[:, pl.ds(0, 128)] = jnp.broadcast_to(row_total[:1], (128, ROWS)).T
-    grads.middle(0, 1)
-    grads.middle(1, 1)
 
     back_sum.arrive()
     sums = [0.0, 0.0, 0.0]
@@ -588,33 +606,28 @@
         for k, term in enumerate((pre_grad * xf, pre_grad, normed_grad * mixed * scaled)):
             sums[k] = sums[k] + jnp.sum(term, axis=0, keepdims=True)
     swap_start(src.at[0], back_cols, *swap(2))
+    out_sum.onward()
     vector_sum = SeqSum(slots, vec_send, vec_recv)
     row, _ = index_pair((8, BLOCK))
     vector_sum.start(
         jnp.where(row == 0, sums[0], jnp.where(row == 1, sums[1], jnp.where(row == 2, sums[2], 0.0)))
     )
-    grads.finish(0)
-    grads.finish(1)
-    grads.multiply(4, flipped, up_back[:, lows])
-    grads.multiply(5, flipped, up_back[:, highs])
+    grads.middle(0, 1)
+    grads.middle(1, 1)
     swap_wait(src.at[0], back_cols, *swap(2))
     src[1] = half(dot(big_two[1], back_cols[...]))
     swap_start(src.at[1], first_back, *swap(3))
     vector_sum.second()
     two_sum = PairSum(two_part, two_got, pair_send.at[0], pair_recv.at[0])
     two_sum.start(gather_two(dot_rows(back_cols[...], first_cols[...])))
+    grads.finish(0)
+    grads.finish(1)
+    grads.middle(4, 0)
+    grads.middle(5, 0)
     grads.turn(2)
     grads.turn(3)
-    grads.middle(4, 0)
-    grads.middle(5, 0)
     two_sum.onward()
     vector_sum.third()
-    out_sum.arrive()
-    plain_out = deal(full(wm[c]) + out_sum.total(pl.ds(0, ROWS)))
-    layer_out[top] = half(plain_out[0])
-    layer_out[low] = half(plain_out[1])
-    grads.middle(2, 1)
-    grads.middle(3, 1)
     swap_wait(src.at[1], first_back, *swap(3))
     one_sum = PairSum(one_part, one_got, pair_send.at[1], pair_recv.at[1])
     blocks = [half(b) for b in deal(full(first_back[...]))]
@@ -623,25 +636,54 @@
             [half(dot_rows(blocks[0], x[top])), half(dot_rows(blocks[1], x[low]))], axis=0
         )
     )
-    kept_plain = deal(gate_pre[:, lows])
+    grads.middle(2, 1)
+    grads.middle(3, 1)
+    kept = deal(gate_pre[:, lows])
     for k, rows in enumerate((top, low)):
-        input_grad[rows] = half(kept_plain[k] + dot(f1[k].T, blocks[k]))
+        hidden[rows, highs] = half(kept[k] + dot(f1[k].T, blocks[k]))
+    outs = [
+        pltpu.make_async_copy(a, b, out_sem.at[UNITS + k])
+        for k, (a, b) in enumerate(
+            (
+                (hidden.at[:, highs], input_grad),
+                (hidden.at[:, lows], layer_out),
+                (up_pre.at[:, pl.ds(BLOCK, 256)], one_grad),
+            )
+        )
+    ]
+    outs[0].start()
+    out_sum.arrive()
+    plain_out = deal(full(wm[c]) + out_sum.total(pl.ds(0, ROWS)))
+    hidden[top, lows] = half(plain_out[0])
+    hidden[low, lows] = half(plain_out[1])
+    outs[1].start()
+    one_sum.onward()
+    grads.turn(4)
+    grads.turn(5)
     grads.finish(2)
     grads.finish(3)
-    one_sum.onward()
-    two_grad[...] = two_sum.finish()
-    vectors[...] = vector_sum.finish()
-    grads.turn(4)
-    grads.turn(5)
     grads.middle(4, 1)
     grads.middle(5, 1)
-    one_grad[...] = one_sum.finish()
+    two_grad[...] = two_sum.finish()
+    vector = vector_sum.finish()
+    scale_grad[...], shift_grad[...], gain_grad[...] = vector[0:1], vector[1:2], vector[2:3]
+    up_pre[:, pl.ds(BLOCK, 256)] = one_sum.finish()
+    outs[2].start()
     for unit in range(4):
         grads.close(unit)
     grads.finish(4)
     grads.finish(5)
     grads.close(4)
     grads.close(5)
+    for copy in outs:
+        copy.wait()
+    for unit in range(UNITS):
+        grads.out_copy(unit).wait()
+
+
+def hand_over(*refs):
+    for src, dst in zip(refs[:OUTPUTS], refs[OUTPUTS:]):
+        dst[...] = src[...]
 
 
 def on_device(
@@ -663,11 +705,15 @@
             out((ROWS, BLOCK), bf),
             out((2 * 256, 256), f32),
             out((ROWS, 64), f32),
-            out((8, BLOCK), f32),
-            out((3, SHARE, HIDDEN), f32),
+            out((1, BLOCK), f32),
+            out((1, BLOCK), f32),
+            out((1, BLOCK), f32),
+            out((SHARE, HIDDEN), f32),
+            out((SHARE, HIDDEN), f32),
+            out((SHARE, HIDDEN), f32),
         ),
         in_specs=[vmem] * 7 + [away] * 3,
-        out_specs=(vmem,) * 6,
+        out_specs=(away,) * 3 + (vmem,) * 4 + (away,) * 3,
         scratch_shapes=[
             pltpu.VMEM((4 * BLOCK, HIDDEN), bf),
             pltpu.VMEM((4 * BLOCK, HIDDEN), bf),
@@ -682,6 +728,7 @@
             pltpu.VMEM((2, 2, ROWS, BLOCK), bf),
             pltpu.VMEM((2, ROWS, BLOCK), bf),
             pltpu.VMEM((SLOTS, 2, 4, 4, SHARE, BLOCK), bf),
+            pltpu.VMEM((SLOTS, 2, 4, SHARE, BLOCK), bf),
             pltpu.VMEM((UNITS, 2, 4, SHARE, BLOCK), bf),
             pltpu.VMEM((UNITS, 2, 2, 4, SHARE, BLOCK), bf),
             pltpu.VMEM((UNITS, 2, SHARE, BLOCK), bf),
@@ -700,6 +747,7 @@
             dma((4,)), dma((4,)),
             dma((2, 2)), dma((2, 2)),
             dma((3, 4)), dma((3, 4)),
+            dma((UNITS + 3,)),
         ],
         compiler_params=pltpu.CompilerParams(
             collective_id=0, has_side_effects=True, vmem_limit_bytes=VMEM_LIMIT
@@ -710,15 +758,25 @@
         gate_scale.reshape(1, -1), gate_shift.reshape(1, -1), norm_gain.reshape(4, 1, -1),
         w_gate, w_up, w_down,
     )
-    layer_out, input_grad, one_grad, two_grad, vectors, grads = outs
+    shapes = [(ROWS, BLOCK, bf), (ROWS, BLOCK, bf), (2 * 256, 256, f32), (ROWS, 64, f32)]
+    shapes = [out(s[:-1], s[-1]) for s in shapes] + [out((1, BLOCK), f32)] * 3
+    shapes += [out((SHARE, HIDDEN), f32)] * 3
+    results = pl.pallas_call(
+        hand_over,
+        out_shape=tuple(shapes),
+        in_specs=[vmem] * OUTPUTS,
+        out_specs=(vmem,) * OUTPUTS,
+        name="hand_over",
+    )(*outs)
+    layer_out, input_grad, one_grad, two_grad, scale_grad, shift_grad, gain_grad, *grads = results
     return (
         layer_out,
         input_grad,
         one_grad.reshape(factor_one.shape),
         two_grad.reshape(factor_two.shape),
-        vectors[0],
-        vectors[1],
-        vectors[2],
+        scale_grad.reshape(-1),
+        shift_grad.reshape(-1),
+        gain_grad.reshape(-1),
         grads[1],
         grads[2],
         grads[0].T,

time: 163 us -> 150 us (0.920)
  local copies, waits for them, and re-layouts: 9.73 us -> 0 us
  Pallas kernels: 149 us -> 147 us
    unnamed x6 -> x0, local copies, waits for them, and re-layouts: 6.31 us -> none
    pallas_call x1, Pallas kernels: 149 us -> 143 us  [on_device(): pl.pallas_call(layer, out_shape=(out((ROWS, BLOCK), bf), out((ROWS, BLOCK...]
    pallas_call x0 -> x1, Pallas kernels: none -> 3.21 us  [on_device(): pl.pallas_call(hand_over, out_shape=tuple(shapes), in_specs=[vmem] * OUTP...]
    transpose x1 -> x0, local copies, waits for them, and re-layouts: 2 us -> none  [on_device(): grads[0]]
where the time goes in v3:
time: 150 us; the launch traced here: 147 us
  Pallas kernels  147 us (98%)
    pallas_call x1, Pallas kernels, on_device(): pl.pallas_call(layer, out_shape=(out((ROWS, BLOCK), bf), out((ROWS, BLOCK...  143 us
    pallas_call x1, Pallas kernels, on_device(): pl.pallas_call(hand_over, out_shape=tuple(shapes), in_specs=[vmem] * OUTP...  3.21 us

profile of v3, /device:TPU:16, one launch (start us, length us, event | category | flops | bytes accessed | tf_op | source)
XLA Modules:
  0.0 147.2 jit_solution(18257893432409521111)
XLA Ops:
  0.6 143.4 %layer.1 = (bf16[512,512]{1,0:T(8,128)(2,1)}, bf16[512,512]{1,0:T(8,128)(2,1)}, f32[512,256]{1,0:T(8,128)}, f32[512,64]{1,0:T(8,128)}, f32[1,512]{1,0:T(1,128)},...) custom-call(bf16[512,512]{1,0:T(8,128)(2,1)} %x.1, ...), custom_call_target="tpu_custom_call" | custom-call | tf_op jit(solution)/shard_map/layer/pallas_call | solution.py:701
  144.0 3.2 %hand_over.1 = (bf16[512,512]{1,0:T(8,128)(2,1)}, bf16[512,512]{1,0:T(8,128)(2,1)}, f32[512,256]{1,0:T(8,128)}, f32[512,64]{1,0:T(8,128)}, f32[1,512]{1,0:T(1,12...) custom-call(bf16[512,512]{1,0:T(8,128)(2,1)} %get-tuple-element.30.r, ...), custom_call_target="tpu_custom_call" | custom-call | tf_op jit(solution)/shard_map/hand_over/pallas_call | solution.py:764

commit v4 on v3

--- a/solution.py
+++ b/solution.py
@@ -13,10 +13,11 @@
 PIECE = ROWS // PIECES
 BLOCK = 512
 HIDDEN = 1024
-UNITS = 6
+UNITS = 10
 SLOTS = 4
 SHARE = 64
 EARLY = 2
+SOON = 2
 OUTPUTS = 10
 VMEM_LIMIT = 67000000
 
@@ -249,82 +250,127 @@
 
 
 class Grads:
-    def __init__(self, own, mid, bufs, sems, result, out, out_sem):
-        self.own, self.mid, self.result = own, mid, result
-        self.out, self.out_sem = out, out_sem
-        self.early_one, self.late_one, self.early_two, self.late_two, self.last = bufs
+    def __init__(self, own, families, got, sems, result, out, out_sem):
+        self.own, self.families, self.got = own, families, got
         self.send, self.recv = sems
+        self.result, self.out, self.out_sem = result, out, out_sem
+        s, c = place()
+        self.near = lax.rem(lax.div(s, 4), 2)
+        self.partner = (s + 4 - 8 * self.near, c)
+
+    def where(self, unit):
+        if unit in (6, 7):
+            return 2, unit - 6
+        return (0, unit) if unit < 2 else (1, unit - 2 if unit < 6 else unit - 4)
 
     def ring(self, unit, stage):
-        slot, first = unit % SLOTS, unit % 2
+        family, k = self.where(unit)
+        early_one, late_one, early_two, late_two, mid = self.families[family][:5]
         sems = [s.at[unit, stage] for s in (self.send, self.recv)]
-        if stage == 0:
-            view = lambda part, owner: self.own.at[slot, part, owner]
-            return Ring(view, self.early_one.at[unit], self.late_one.at[unit], *sems, first)
-        view = lambda part, owner: self.mid.at[slot, part, owner]
-        return Ring(view, self.early_two.at[unit], self.late_two.at[unit], *sems, 1 - first)
-
-    def multiply(self, unit, left, right):
-        slot = unit % SLOTS
+        first, own = unit % 2, self.own
+        if stage == 1:
+            view = lambda part, owner: mid.at[k, part, owner]
+            return Ring(view, early_two.at[k], late_two.at[k], *sems, 1 - first)
+        cols = pl.ds(k % 2 * 256, 256)
+        if family == 0:
+            view = lambda part, owner: own.at[2 + unit, part, owner]
+        elif family == 1:
+            view = lambda part, owner: own.at[1 + k // 4 * 2, part, owner, :, :, cols]
+        elif first == 0:
+            view = lambda part, owner: own.at[0, self.near, :, owner, pl.ds(part * 32, 32), cols]
+        else:
+            view = lambda part, owner: own.at[0, self.near, owner, :, pl.ds(part * 32, 32), cols]
+        return Ring(view, early_one.at[k], late_one.at[k], *sems, first)
+
+    def multiply(self, slot, left, right, mode):
         own = self.own
         for z in range(4):
             tile = half(dot(left[pl.ds(z * 512, 512), :], right).reshape(2, 4, SHARE, BLOCK))
-            if unit % 2 == 0:
+            if mode == 0:
                 own[slot, :, :, z] = tile
+            elif mode == 1:
+                own[slot, :, z] = tile
             else:
-                own[slot, :, z] = tile
-
+                own[slot, :, :, z, :, pl.ds(0, 256)] = tile[..., :256]
+                own[slot, :, z, :, :, pl.ds(256, 256)] = tile[..., 256:]
+
+    def start(self, unit):
         self.ring(unit, 0).start()
 
     def middle(self, unit, stage):
         self.ring(unit, stage).middle()
 
+    def meet_copy(self):
+        src = self.own.at[0, 1 - self.near]
+        return remote(src, self.got, self.send.at[6, 2, 0], self.recv.at[6, 2, 0], self.partner)
+
+    def meet(self):
+        self.meet_copy().wait()
+
+        @pl.loop(0, 4)
+        def _(z):
+            mine = self.own.at[0, self.near, z]
+            mine[...] = half(full(mine[...]) + full(self.got[z]))
+
+        self.start(6)
+        self.start(7)
+
     def turn(self, unit):
+        family, k = self.where(unit)
+        mid = self.families[family][4]
         ring = self.ring(unit, 0)
         ring.arrive()
-        if unit >= SLOTS:
-            self.last_copy(unit - SLOTS).wait_send()
 
         @pl.loop(0, 2)
         def _(part):
-            self.mid[unit % SLOTS, part] = half(ring.total(part))
+            mid[k, part] = half(ring.total(part))
 
         self.ring(unit, 1).start()
         ring.settle()
 
     def last_copy(self, unit):
-        s, c = place()
-        near = lax.rem(lax.div(s, 4), 2)
+        family, k = self.where(unit)
         ring = self.ring(unit, 1)
         sems = [s.at[unit, 2, 0] for s in (self.send, self.recv)]
-        src = ring.view(1 - near, ring.here)
-        return remote(src, self.last.at[unit], *sems, (s + 4 - 8 * near, c))
+        src = ring.view(1 - self.near, ring.here)
+        return remote(src, self.families[family][5].at[k], *sems, self.partner)
 
     def finish(self, unit):
-        s, _ = place()
-        near = lax.rem(lax.div(s, 4), 2)
         ring = self.ring(unit, 1)
         ring.arrive()
-        ring.view(1 - near, ring.here)[...] = half(ring.total(1 - near))
-        self.last_copy(unit).start()
-        self.result[self.place(unit)] = ring.total(near)
+        if unit not in (6, 7):
+            ring.view(1 - self.near, ring.here)[...] = half(ring.total(1 - self.near))
+            self.last_copy(unit).start()
+            self.result[self.place(unit)] = ring.total(self.near)
+        else:
+            rows, cols = self.place(unit)
+            for part in range(2):
+                self.result[pl.ds(rows.start + part * 32, 32), cols] = ring.total(part)
+            self.out_copy(unit).start()
         ring.settle()
 
+    def close(self, unit):
+        family, k = self.where(unit)
+        self.last_copy(unit).wait()
+        place = self.place(unit)
+        self.result[place] = self.result[place] + full(self.families[family][5][k])
+        self.out_copy(unit).start()
+
     def place(self, unit):
-        return pl.ds(unit * SHARE, SHARE), pl.ds(BLOCK, BLOCK)
+        family, k = self.where(unit)
+        if family == 0:
+            return pl.ds(unit * SHARE, SHARE), pl.ds(BLOCK, BLOCK)
+        block = 5 if family == 2 else 2 + k // 2
+        return pl.ds(block * SHARE, SHARE), pl.ds(BLOCK + k % 2 * 256, 256)
 
     def out_copy(self, unit):
-        cols = pl.ds(unit % 2 * BLOCK, BLOCK)
-        dst = self.out[unit // 2].at[:, cols]
+        family, k = self.where(unit)
+        if family == 0:
+            dst = self.out[1].at[:, pl.ds(k * BLOCK, BLOCK)]
+        else:
+            which, base = (0, 0) if family == 2 else ((2, 0), (0, BLOCK), (2, BLOCK))[k // 2]
+            dst = self.out[which].at[:, pl.ds(base + k % 2 * 256, 256)]
         return pltpu.make_async_copy(self.result.at[self.place(unit)], dst, self.out_sem.at[unit])
-
-    def close(self, unit):
-        self.last_copy(unit).wait_recv()
-        if unit + SLOTS >= UNITS:
-            self.last_copy(unit).wait_send()
-        place = self.place(unit)
-        self.result[place] = self.result[place] + full(self.last[unit])
-        self.out_copy(unit).start()
 
 
 class ChanSum:
@@ -443,7 +489,10 @@
     layer_out, input_grad, one_grad, two_grad, scale_grad, shift_grad, gain_grad, down_out, gate_out, up_out,
     wg, wu, wd, cot, flipped, wm, normed, gate_pre, up_pre, hidden, gate_back, up_back,
     inv, dots, first_cols, seqmix, back_cols, first_back, src, big_two,
-    sum_near, sum_far, own, mid, early_one, late_one, early_two, late_two, last,
+    sum_near, sum_far, own, got,
+    early_one, late_one, early_two, late_two, mid, last,
+    early_one5, late_one5, early_two5, late_two5, mid5, last5,
+    early_one4, late_one4, early_two4, late_two4, mid4,
     one_part, one_got, two_part, two_got, slots,
     w_sem, swap_send, swap_recv, gs, gr, hs, hr, grad_send, grad_recv, sum_send, sum_recv,
     dot_send, dot_recv, pair_send, pair_recv, vec_send, vec_recv, out_sem,
@@ -471,6 +520,8 @@
     swap_wait(src.at[0], first_cols, *swap(0))
     src[1] = half(dot(big_two[0], first_cols[...]))
     swap_start(src.at[1], seqmix, *swap(1))
+    for piece in range(EARLY, SOON):
+        gather_start(cot, piece, hs, hr)
     for piece in range(EARLY):
         gather_forward(cot, piece, hs, hr)
     swap_wait(src.at[1], seqmix, *swap(1))
@@ -480,8 +531,10 @@
         opening = jax.nn.sigmoid(xf * scale[...] + shift[...])
         wm[c, rows] = half(xf + opening * full(seqmix[rows]))
         gather_start(wm, piece, gs, gr)
-    for piece in range(EARLY, PIECES):
+    for piece in range(SOON, PIECES):
         gather_start(cot, piece, hs, hr)
+    for piece in range(EARLY, SOON):
+        gather_forward(cot, piece, hs, hr)
     for piece in range(PIECES):
         gather_forward(wm, piece, gs, gr)
     for copy in weights:
@@ -517,19 +570,29 @@
     expand(0, 1)
     norm_rows(1)
     expand(1, 0)
-    for piece in range(EARLY, PIECES):
+    for piece in range(SOON, PIECES):
         gather_forward(cot, piece, hs, hr)
     for piece in range(PIECES):
         gather_finish(cot, piece, hs, hr)
     for k in range(4):
         flipped[pl.ds(k * BLOCK, BLOCK), :] = cot[k].T
     grads = Grads(
-        own, mid, (early_one, late_one, early_two, late_two, last), (grad_send, grad_recv),
+        own,
+        (
+            (early_one, late_one, early_two, late_two, mid, last),
+            (early_one5, late_one5, early_two5, late_two5, mid5, last5),
+            (early_one4, late_one4, early_two4, late_two4, mid4),
+        ),
+        got,
+        (grad_send, grad_recv),
         gate_pre, (down_out, gate_out, up_out), out_sem,
     )
-    grads.multiply(0, flipped, hidden[:, lows])
+    grads.multiply(0, flipped, hidden[:, lows], 1)
+    grads.meet_copy().start()
     expand(1, 1)
-    grads.multiply(1, flipped, hidden[:, highs])
+    grads.multiply(1, flipped, hidden[:, highs], 2)
+    grads.start(4)
+    grads.start(5)
     for k in range(4):
         flipped[pl.ds(k * BLOCK, BLOCK), :] = normed[k].T
 
@@ -558,10 +621,12 @@
     ]
     for copy in dot_copies:
         copy.start()
-    grads.middle(0, 0)
-    grads.middle(1, 0)
-    grads.multiply(2, flipped, gate_back[:, lows])
-    grads.multiply(3, flipped, gate_back[:, highs])
+    grads.middle(4, 0)
+    grads.middle(5, 0)
+    grads.multiply(2, flipped, gate_back[:, lows], 0)
+    grads.start(0)
+    grads.multiply(3, flipped, gate_back[:, highs], 1)
+    grads.start(1)
 
     @pl.loop(0, 4)
     def _(chan):
@@ -573,22 +638,32 @@
         normed, sum_near.at[0], sum_far.at[0], sum_send.at[0], sum_recv.at[0]
     )
     back_sum.start()
+    grads.turn(4)
+    grads.turn(5)
+    grads.multiply(1, flipped, up_back[:, lows], 2)
+    grads.start(2)
+    grads.start(3)
+    back_sum.onward()
+    grads.middle(0, 0)
+    grads.middle(1, 0)
     for chan in range(4):
         cols = pl.ds(chan * BLOCK, BLOCK)
         cot[chan] = half(dot(hidden[...], wd[:, cols]))
-    back_sum.onward()
     out_sum = ChanSum(cot, sum_near.at[1], sum_far.at[1], sum_send.at[1], sum_recv.at[1])
     out_sum.start()
-    grads.turn(0)
-    grads.turn(1)
-    grads.multiply(4, flipped, up_back[:, lows])
-    grads.multiply(5, flipped, up_back[:, highs])
-    grads.middle(2, 0)
-    grads.middle(3, 0)
     for copy in dot_copies:
         copy.wait()
     row_total = (dots[0] + dots[1]) + (dots[2] + dots[3])
     up_pre[:, pl.ds(0, 128)] = jnp.broadcast_to(row_total[:1], (128, ROWS)).T
+    grads.meet()
+    grads.middle(4, 1)
+    grads.middle(5, 1)
+    grads.turn(1)
+    grads.multiply(3, flipped, up_back[:, highs], 2)
+    grads.start(8)
+    grads.start(9)
+    grads.middle(2, 0)
+    grads.middle(3, 0)
 
     back_sum.arrive()
     sums = [0.0, 0.0, 0.0]
@@ -612,22 +687,46 @@
     vector_sum.start(
         jnp.where(row == 0, sums[0], jnp.where(row == 1, sums[1], jnp.where(row == 2, sums[2], 0.0)))
     )
-    grads.middle(0, 1)
-    grads.middle(1, 1)
+    grads.middle(6, 0)
+    grads.middle(7, 0)
+    grads.finish(4)
+    grads.finish(5)
+    grads.turn(0)
+    grads.middle(8, 0)
+    grads.middle(9, 0)
     swap_wait(src.at[0], back_cols, *swap(2))
     src[1] = half(dot(big_two[1], back_cols[...]))
     swap_start(src.at[1], first_back, *swap(3))
     vector_sum.second()
     two_sum = PairSum(two_part, two_got, pair_send.at[0], pair_recv.at[0])
     two_sum.start(gather_two(dot_rows(back_cols[...], first_cols[...])))
-    grads.finish(0)
-    grads.finish(1)
-    grads.middle(4, 0)
-    grads.middle(5, 0)
+    grads.middle(1, 1)
+    grads.turn(6)
+    grads.turn(7)
+    grads.middle(0, 1)
     grads.turn(2)
     grads.turn(3)
+    grads.close(4)
+    grads.close(5)
+    out_sum.arrive()
+    plain_out = deal(full(wm[c]) + out_sum.total(pl.ds(0, ROWS)))
+    hidden[top, lows] = half(plain_out[0])
+    hidden[low, lows] = half(plain_out[1])
+    outs = [
+        pltpu.make_async_copy(a, b, out_sem.at[UNITS + k])
+        for k, (a, b) in enumerate(
+            (
+                (hidden.at[:, highs], input_grad),
+                (hidden.at[:, lows], layer_out),
+                (up_pre.at[:, pl.ds(BLOCK, 256)], one_grad),
+            )
+        )
+    ]
+    outs[1].start()
     two_sum.onward()
     vector_sum.third()
+    grads.turn(8)
+    grads.turn(9)
     swap_wait(src.at[1], first_back, *swap(3))
     one_sum = PairSum(one_part, one_got, pair_send.at[1], pair_recv.at[1])
     blocks = [half(b) for b in deal(full(first_back[...]))]
@@ -638,43 +737,30 @@
     )
     grads.middle(2, 1)
     grads.middle(3, 1)
+    grads.middle(8, 1)
+    grads.middle(9, 1)
     kept = deal(gate_pre[:, lows])
     for k, rows in enumerate((top, low)):
         hidden[rows, highs] = half(kept[k] + dot(f1[k].T, blocks[k]))
-    outs = [
-        pltpu.make_async_copy(a, b, out_sem.at[UNITS + k])
-        for k, (a, b) in enumerate(
-            (
-                (hidden.at[:, highs], input_grad),
-                (hidden.at[:, lows], layer_out),
-                (up_pre.at[:, pl.ds(BLOCK, 256)], one_grad),
-            )
-        )
-    ]
     outs[0].start()
-    out_sum.arrive()
-    plain_out = deal(full(wm[c]) + out_sum.total(pl.ds(0, ROWS)))
-    hidden[top, lows] = half(plain_out[0])
-    hidden[low, lows] = half(plain_out[1])
-    outs[1].start()
     one_sum.onward()
-    grads.turn(4)
-    grads.turn(5)
-    grads.finish(2)
-    grads.finish(3)
-    grads.middle(4, 1)
-    grads.middle(5, 1)
+    grads.middle(6, 1)
+    grads.middle(7, 1)
+    grads.finish(0)
+    grads.finish(1)
     two_grad[...] = two_sum.finish()
     vector = vector_sum.finish()
     scale_grad[...], shift_grad[...], gain_grad[...] = vector[0:1], vector[1:2], vector[2:3]
+    grads.finish(2)
+    grads.finish(3)
+    grads.finish(8)
+    grads.finish(9)
+    grads.finish(6)
+    grads.finish(7)
     up_pre[:, pl.ds(BLOCK, 256)] = one_sum.finish()
     outs[2].start()
-    for unit in range(4):
+    for unit in (0, 1, 2, 3, 8, 9):
         grads.close(unit)
-    grads.finish(4)
-    grads.finish(5)
-    grads.close(4)
-    grads.close(5)
     for copy in outs:
         copy.wait()
     for unit in range(UNITS):
@@ -728,12 +814,24 @@
             pltpu.VMEM((2, 2, ROWS, BLOCK), bf),
             pltpu.VMEM((2, ROWS, BLOCK), bf),
             pltpu.VMEM((SLOTS, 2, 4, 4, SHARE, BLOCK), bf),
-            pltpu.VMEM((SLOTS, 2, 4, SHARE, BLOCK), bf),
-            pltpu.VMEM((UNITS, 2, 4, SHARE, BLOCK), bf),
-            pltpu.VMEM((UNITS, 2, 2, 4, SHARE, BLOCK), bf),
-            pltpu.VMEM((UNITS, 2, SHARE, BLOCK), bf),
-            pltpu.VMEM((UNITS, 2, 2, SHARE, BLOCK), bf),
-            pltpu.VMEM((UNITS, SHARE, BLOCK), bf),
+            pltpu.VMEM((4, 4, SHARE, BLOCK), bf),
+            pltpu.VMEM((2, 2, 4, SHARE, BLOCK), bf),
+            pltpu.VMEM((2, 2, 2, 4, SHARE, BLOCK), bf),
+            pltpu.VMEM((2, 2, SHARE, BLOCK), bf),
+            pltpu.VMEM((2, 2, 2, SHARE, BLOCK), bf),
+            pltpu.VMEM((2, 2, 4, SHARE, BLOCK), bf),
+            pltpu.VMEM((2, SHARE, BLOCK), bf),
+            pltpu.VMEM((6, 2, 4, SHARE, 256), bf),
+            pltpu.VMEM((6, 2, 2, 4, SHARE, 256), bf),
+            pltpu.VMEM((6, 2, SHARE, 256), bf),
+            pltpu.VMEM((6, 2, 2, SHARE, 256), bf),
+            pltpu.VMEM((6, 2, 4, SHARE, 256), bf),
+            pltpu.VMEM((6, SHARE, 256), bf),
+            pltpu.VMEM((2, 2, 4, SHARE // 2, 256), bf),
+            pltpu.VMEM((2, 2, 2, 4, SHARE // 2, 256), bf),
+            pltpu.VMEM((2, 2, SHARE // 2, 256), bf),
+            pltpu.VMEM((2, 2, 2, SHARE // 2, 256), bf),
+            pltpu.VMEM((2, 2, 4, SHARE // 2, 256), bf),
             pltpu.VMEM((2, 2 * 256, 256), bf),
             pltpu.VMEM((2, 2 * 256, 256), bf),
             pltpu.VMEM((2, ROWS, 64), bf),

time: 150 us -> 146 us (0.973); the launches traced: 147 us -> 145 us
  Pallas kernels: 147 us -> 144 us
    pallas_call x1, Pallas kernels: 143 us -> 141 us  [on_device(): pl.pallas_call(layer, out_shape=(out((ROWS, BLOCK), bf), out((ROWS, BLOCK...]
where the time goes in v4:
time: 146 us; the launch traced here: 145 us
  Pallas kernels  144 us (99%)
    pallas_call x1, Pallas kernels, on_device(): pl.pallas_call(layer, out_shape=(out((ROWS, BLOCK), bf), out((ROWS, BLOCK...  141 us
    pallas_call x1, Pallas kernels, on_device(): pl.pallas_call(hand_over, out_shape=tuple(shapes), in_specs=[vmem] * OUTP...  3.21 us

profile of v4, /device:TPU:16, one launch (start us, length us, event | category | flops | bytes accessed | tf_op | source)
XLA Modules:
  0.0 145.1 jit_solution(1332042938655635597)
XLA Ops:
  0.6 141.3 %layer.1 = (bf16[512,512]{1,0:T(8,128)(2,1)}, bf16[512,512]{1,0:T(8,128)(2,1)}, f32[512,256]{1,0:T(8,128)}, f32[512,64]{1,0:T(8,128)}, f32[1,512]{1,0:T(1,128)},...) custom-call(bf16[512,512]{1,0:T(8,128)(2,1)} %x.1, ...), custom_call_target="tpu_custom_call" | custom-call | tf_op jit(solution)/shard_map/layer/pallas_call | solution.py:787
  141.9 3.2 %hand_over.1 = (bf16[512,512]{1,0:T(8,128)(2,1)}, bf16[512,512]{1,0:T(8,128)(2,1)}, f32[512,256]{1,0:T(8,128)}, f32[512,64]{1,0:T(8,128)}, f32[1,512]{1,0:T(1,12...) custom-call(bf16[512,512]{1,0:T(8,128)(2,1)} %get-tuple-element.30.r, ...), custom_call_target="tpu_custom_call" | custom-call | tf_op jit(solution)/shard_map/hand_over/pallas_call | solution.py:862

commit v5 on v4

--- a/solution.py
+++ b/solution.py
@@ -768,8 +768,21 @@
 
 
 def hand_over(*refs):
-    for src, dst in zip(refs[:OUTPUTS], refs[OUTPUTS:]):
-        dst[...] = src[...]
+    ins, outs = refs[:OUTPUTS], refs[OUTPUTS : 2 * OUTPUTS]
+    held, sems = refs[2 * OUTPUTS : -1], refs[-1]
+    taken = [
+        pltpu.make_async_copy(a, b, sems.at[0, k]) for k, (a, b) in enumerate(zip(ins, held))
+    ]
+    given = [
+        pltpu.make_async_copy(a, b, sems.at[1, k]) for k, (a, b) in enumerate(zip(held, outs))
+    ]
+    for copy in taken:
+        copy.start()
+    for first, second in zip(taken, given):
+        first.wait()
+        second.start()
+    for copy in given:
+        copy.wait()
 
 
 def on_device(
@@ -862,8 +875,9 @@
     results = pl.pallas_call(
         hand_over,
         out_shape=tuple(shapes),
-        in_specs=[vmem] * OUTPUTS,
-        out_specs=(vmem,) * OUTPUTS,
+        in_specs=[away] * OUTPUTS,
+        out_specs=(away,) * OUTPUTS,
+        scratch_shapes=[pltpu.VMEM(s.shape, s.dtype) for s in shapes] + [dma((2, OUTPUTS))],
         name="hand_over",
     )(*outs)
     layer_out, input_grad, one_grad, two_grad, scale_grad, shift_grad, gain_grad, *grads = results

time: 146 us -> 146 us (level)
  no operation moved by 1% of the time
where the time goes in v5:
time: 146 us; the launch traced here: 145 us
  Pallas kernels  144 us (99%)
    pallas_call x1, Pallas kernels, on_device(): pl.pallas_call(layer, out_shape=(out((ROWS, BLOCK), bf), out((ROWS, BLOCK...  141 us

profile of v5, /device:TPU:16, one launch (start us, length us, event | category | flops | bytes accessed | tf_op | source)
XLA Modules:
  0.0 144.8 jit_solution(209611797773392767)
XLA Ops:
  0.6 141.3 %layer.1 = (bf16[512,512]{1,0:T(8,128)(2,1)}, bf16[512,512]{1,0:T(8,128)(2,1)}, f32[512,256]{1,0:T(8,128)}, f32[512,64]{1,0:T(8,128)}, f32[1,512]{1,0:T(1,128)},...) custom-call(bf16[512,512]{1,0:T(8,128)(2,1)} %x.1, ...), custom_call_target="tpu_custom_call" | custom-call | tf_op jit(solution)/shard_map/layer/pallas_call | solution.py:800
  141.9 2.7 %hand_over.1 = (bf16[512,512]{1,0:T(8,128)(2,1)}, bf16[512,512]{1,0:T(8,128)(2,1)}, f32[512,256]{1,0:T(8,128)}, f32[512,64]{1,0:T(8,128)}, f32[1,512]{1,0:T(1,12...) custom-call(bf16[512,512]{1,0:T(8,128)(2,1)} %get-tuple-element.30.r, ...), custom_call_target="tpu_custom_call" | custom-call | tf_op jit(solution)/shard_map/hand_over/pallas_call | solution.py:875
